TPU v7x, 32 devices: a whole 2x2x4 slice. The times are simulated.
32 devices in a mesh: strip: 2 (over x), az: 4 (over z), tile: 4 (over y, core).
Axes of the slice: x: 2, y: 2, z: 4, core: 2. Of those that a mesh axis runs over, the one named last changes fastest.
Arguments:
- raw_echo: float32 [2, 4096, 4096], P(None, ('strip', 'az', 'tile')), parts along dimension 1, may hold values from -6 to 6
- phase_scaling: float32 [1024, 4096], P(None, 'tile'), may hold values from -3.140625 to 3.140625
- phase_range: float32 [1024, 4096], P('tile'), may hold values from -3.140625 to 3.140625
- phase_azimuth: float32 [1024, 4096], P(None, 'tile'), may hold values from -3.140625 to 3.140625
Outputs:
- image: float32 [2, 4096, 4096], P(None, ('strip', 'az'), 'tile'), parts along dimension 1
There are 2 independent parts, one for each index of `strip`. A program takes and returns all parts, laid end to end along the dimension named above; an argument that names none is the same for every part. Nothing has to cross between parts.
All inputs are finite; a program needn't handle non-finite values.
Results may differ from a plain program's by a relative error of at most 0.00007.
Values sent between devices are 32-bit elements; how exact they have to be, the bound alone decides.
No kernel may reach another device: no remote copies, remote signals or barrier semaphores. Data moves between devices by JAX's collectives and lax.ppermute only.
A program may use at most 128 MiB of HBM per device.

v0:
```python
import math

import jax
import jax.numpy as jnp
from jax import lax
from jax.sharding import PartitionSpec as P


def from_behind(value, axis, by):
    length = lax.axis_size(axis)
    pairs = [(i, i + by) for i in range(length) if 0 <= i + by < length]
    return lax.ppermute(value, axis, pairs)


def split_length(extent):
    return (extent // 128, 128)


def unit_roots(row_lo, row_hi, col_count, modulus, direction):
    row_index = jnp.arange(row_lo, row_hi, dtype=jnp.int32)
    col_index = jnp.arange(col_count, dtype=jnp.int32)
    residue = row_index[:, None] * col_index[None, :] % modulus
    phase_angle = residue.astype(jnp.float32) * (direction * 2.0 * math.pi / modulus)
    return (jnp.cos(phase_angle), jnp.sin(phase_angle))


def complex_mix(spec, table, values):

    def mixing(left, right):
        return jnp.einsum(spec, left, right, precision=lax.Precision.HIGHEST)

    return (
        mixing(table[0], values[0]) - mixing(table[1], values[1]),
        mixing(table[0], values[1]) + mixing(table[1], values[0]),
    )


def rotate(values, table):
    return (
        values[0] * table[0] - values[1] * table[1],
        values[0] * table[1] + values[1] * table[0],
    )


def azimuth_front(values, direction):
    extent, width = values[0].shape
    n_one, n_two = split_length(extent)
    shaped = (values[0].reshape(n_one, n_two, width), values[1].reshape(n_one, n_two, width))
    sectioned = complex_mix("ka,abc->kbc", unit_roots(0, n_one, n_one, n_one, direction), shaped)
    twist = unit_roots(0, n_one, n_two, extent, direction)
    return rotate(sectioned, (twist[0][:, :, None], twist[1][:, :, None]))


def azimuth_back(sectioned, direction, row_lo, row_hi):
    n_one, n_two, width = sectioned[0].shape
    table = unit_roots(row_lo, row_hi, n_two, n_two, direction)
    mixed = complex_mix("mb,kbc->mkc", table, sectioned)
    row_count = (row_hi - row_lo) * n_one
    return (mixed[0].reshape(row_count, width), mixed[1].reshape(row_count, width))


def range_forward(values):
    width, extent = values[0].shape
    n_one, n_two = split_length(extent)
    shaped = (values[0].reshape(width, n_one, n_two), values[1].reshape(width, n_one, n_two))
    sectioned = complex_mix("ka,cab->ckb", unit_roots(0, n_one, n_one, n_one, -1.0), shaped)
    sectioned = rotate(sectioned, unit_roots(0, n_one, n_two, extent, -1.0))
    mixed = complex_mix("mb,ckb->ckm", unit_roots(0, n_two, n_two, n_two, -1.0), sectioned)
    return (mixed[0].reshape(width, extent), mixed[1].reshape(width, extent))


def range_inverse(values):
    width, extent = values[0].shape
    n_one, n_two = split_length(extent)
    shaped = (values[0].reshape(width, n_one, n_two), values[1].reshape(width, n_one, n_two))
    sectioned = complex_mix("mb,ckm->ckb", unit_roots(0, n_two, n_two, n_two, 1.0), shaped)
    sectioned = rotate(sectioned, unit_roots(0, n_one, n_two, extent, 1.0))
    mixed = complex_mix("ka,ckb->cab", unit_roots(0, n_one, n_one, n_one, 1.0), sectioned)
    scale = 1.0 / extent
    return (mixed[0].reshape(width, extent) * scale, mixed[1].reshape(width, extent) * scale)


def body(raw_echo, phase_scaling, phase_range, phase_azimuth):
    tile_count = lax.axis_size("tile")
    columns = lax.all_to_all(raw_echo, "tile", split_axis=2, concat_axis=1, tiled=True)
    pulse_count = columns.shape[1]
    width = columns.shape[2]
    extent = phase_scaling.shape[0]
    tail_count = extent - pulse_count
    padded = jnp.pad(columns, ((0, 0), (0, tail_count), (0, 0)))
    forward = azimuth_front((padded[0], padded[1]), -1.0)
    spectrum = azimuth_back(forward, -1.0, 0, forward[0].shape[1])
    spectrum = rotate(spectrum, (jnp.cos(phase_scaling), jnp.sin(phase_scaling)))
    grouped = jnp.stack(spectrum).reshape(2, tile_count, extent // tile_count, width)
    doppler = lax.all_to_all(grouped, "tile", split_axis=1, concat_axis=3, tiled=True)
    row_count = doppler.shape[2]
    range_count = doppler.shape[3]
    r_one, r_two = split_length(range_count)
    spectral = range_forward((doppler[0, 0], doppler[1, 0]))
    permuted = (
        phase_range.reshape(row_count, r_two, r_one)
        .transpose(0, 2, 1)
        .reshape(row_count, range_count)
    )
    spectral = rotate(spectral, (jnp.cos(permuted), jnp.sin(permuted)))
    filtered = range_inverse(spectral)
    returned = lax.all_to_all(
        jnp.stack(filtered)[:, None], "tile", split_axis=3, concat_axis=1, tiled=True
    )
    returned = returned.reshape(2, extent, width)
    compressed = rotate(
        (returned[0], returned[1]), (jnp.cos(phase_azimuth), jnp.sin(phase_azimuth))
    )
    sectioned = azimuth_front(compressed, 1.0)
    a_one = sectioned[0].shape[0]
    a_two = sectioned[0].shape[1]
    scale = 1.0 / extent
    tail_lo = pulse_count // a_one
    head_hi = -(-pulse_count // a_one)
    tail_part = azimuth_back(sectioned, 1.0, tail_lo, a_two)
    offset = pulse_count - tail_lo * a_one
    tail_block = jnp.stack(tail_part) * scale
    incoming = from_behind(tail_block, "az", 1)
    head_part = azimuth_back(sectioned, 1.0, 0, head_hi)
    head_block = jnp.stack(head_part) * scale
    return jnp.concatenate([head_block + incoming, head_block[:, tail_count:]], axis=1)


def solution(mesh):
    return jax.shard_map(
        body,
        mesh=mesh,
        in_specs=(
            P(None, ("strip", "az", "tile"), None),
            P(None, "tile"),
            P("tile", None),
            P(None, "tile"),
        ),
        out_specs=P(None, ("strip", "az"), "tile"),
        check_vma=False,
    )
```

profile of v0, /device:TPU:0, one launch (start us, length us, event | category | flops | bytes accessed | tf_op | source)
XLA Modules:
  0.0 706.2 jit_solution(165255690241581472)
XLA Ops:
  12.4 16.6 %fusion.398 = (f32[1024,1024]{1,0:T(8,128)}, f32[1024,1024]{1,0:T(8,128)}) fusion(f32[1024,1024]{1,0:T(8,128)} %param.5), kind=kLoop, calls=%fused_computation.414 | loop fusion | bytes 12582912 | tf_op jit(solution)/shard_map/sin | solution.py:93
  29.0 32.0 %all-to-all-done = f32[2,128,4096]{1,0,2:T(2,128)} async-done(((f32[2,128,4096]{1,0,2:T(2,128)}), f32[2,128,4096]{1,0,2:T(2,128)}, u32[]{:S(2)}, u32[]{:S(2)}) %all-to-all-start) | async-done | bytes 4194336 | tf_op jit(solution)/shard_map/all_to_all | solution.py:85
  93.4 7.4 %multiply_subtract_fusion.2 = (f32[8,128,1024]{2,0,1:T(8,128)S(1)}, f32[8,128,1024]{2,0,1:T(8,128)S(1)}) fusion(f32[8,128,1024]{2,0,1:T(8,128)S(1)} %fusion.65, f32[8,128]{0,1:T(8,128)S(1)} %copy.189, f32[8,128]{0,1:T(8,128)S(1)} %copy.186, f32[8,128,1024]{2,0,1:T(8,128)S(1)} %fusion.41, f32[8,128,1024]{2,1,0:T(8,128)S(1)} %bitcast.205), kind=kOutput, calls=%fused_computation.38 | convolution fusion | flops 108004224 | bytes 20979712 | tf_op jit(solution)/shard_map/ka,abc->kbc/dot_general | solution.py:30
  126.2 9.6 %fusion.7 = (f32[1024,1024]{1,0:T(8,128)S(1)}, f32[1024,1024]{1,0:T(8,128)S(1)}) fusion(f32[1024,1024]{1,0:T(8,128)S(1)} %copy-done.7, f32[1024,1024]{1,0:T(8,128)S(1)} %copy-done.8, f32[128,8,1024]{2,0,1:T(8,128)S(1)} %fusion.74, f32[128,8,1024]{2,0,1:T(8,128)S(1)} %fusion.71), kind=kLoop, calls=%fused_computation.27 | loop fusion | flops 6291456 | bytes 25165824 | tf_op jit(solution)/shard_map/sub | solution.py:40
  151.4 16.6 %fusion.397 = (f32[256,4096]{0,1:T(8,128)}, f32[256,4096]{0,1:T(8,128)}) fusion(f32[256,4096]{0,1:T(8,128)} %copy.206), kind=kLoop, calls=%fused_computation.413 | loop fusion | bytes 12582912 | tf_op jit(solution)/shard_map/cos | solution.py:105
  178.7 60.2 %all-to-all-done.1 = f32[2,4,256,1024]{3,2,0,1:T(8,128)} async-done(((f32[2,4,256,1024]{3,2,0,1:T(8,128)}), f32[2,4,256,1024]{3,2,0,1:T(8,128)}, u32[]{:S(2)}, u32[]{:S(2)}) %all-to-all-start.1) | async-done | bytes 8388640 | tf_op jit(solution)/shard_map/all_to_all | solution.py:95
  256.0 8.1 %fusion.180 = f32[256,128,32]{1,2,0:T(8,128)} fusion(f32[256,32,128]{2,1,0:T(8,128)} %reshape_squeeze.14), kind=kOutput, calls=%fused_computation.197 | convolution fusion | flops 402667520 | bytes 8388608 | tf_op jit(solution)/shard_map/ka,cab->ckb/dot_general | solution.py:30
  296.3 8.7 %fusion.25 = f32[256,32,128]{2,0,1:T(8,128)} fusion(f32[256,32,128]{2,1,0:T(8,128)S(1)} %get-tuple-element.18), kind=kOutput, calls=%fused_computation.55 | convolution fusion | flops 1610842112 | bytes 8388608 | tf_op jit(solution)/shard_map/mb,ckb->ckm/dot_general | solution.py:30
  311.9 9.6 %fusion.3 = (f32[256,32,128]{2,0,1:T(8,128)S(1)}, f32[256,32,128]{2,0,1:T(8,128)S(1)}) fusion(f32[256,128,32]{1,0,2:T(8,128)S(1)} %copy-done.5, f32[256,32,128]{2,0,1:T(8,128)S(1)} %fusion.77, f32[256,128,32]{1,0,2:T(8,128)S(1)} %copy-done.4, f32[256,32,128]{2,0,1:T(8,128)} %fusion.25, f32[256,32,128]{2,1,0:T(8,128)S(1)} %get-tuple-element.17), kind=kOutput, calls=%fused_computation.15 | convolution fusion | flops 1618182144 | bytes 29360128 | tf_op jit(solution)/shard_map/mb,ckb->ckm/dot_general | solution.py:30
  343.5 9.1 %fusion.17 = f32[256,128,32]{1,2,0:T(8,128)} fusion(f32[256,32,128]{2,0,1:T(8,128)S(1)} %get-tuple-element.16), kind=kOutput, calls=%fused_computation.47 | convolution fusion | flops 402667520 | bytes 8388608 | tf_op jit(solution)/shard_map/ka,ckb->cab/dot_general | solution.py:30
  352.7 9.1 %multiply_bitcast_fusion.1 = f32[256,32,128]{2,1,0:T(8,128)} fusion(f32[256,128,32]{1,2,0:T(8,128)S(1)} %fusion.19, f32[256,32,128]{2,0,1:T(8,128)S(1)} %get-tuple-element.15), kind=kOutput, calls=%fused_computation.34 | convolution fusion | flops 404764672 | bytes 12582912 | tf_op jit(solution)/shard_map/ka,ckb->cab/dot_general | solution.py:30
  366.7 10.4 %copy.216 = f32[1,256,4096]{1,0,2:T(1,128)} copy(f32[1,256,4096]{2,1,0:T(8,128)} %mul.871) | data formatting | bytes 8388608 | tf_op jit(solution)/shard_map/mul | solution.py:80
  377.2 11.8 %multiply_bitcast_fusion = f32[256,32,128]{2,1,0:T(8,128)} fusion(f32[256,128,32]{1,2,0:T(8,128)} %fusion.17, f32[256,32,128]{2,0,1:T(8,128)} %copy-done), kind=kOutput, calls=%fused_computation.33 | convolution fusion | flops 404764672 | bytes 12582912 | tf_op jit(solution)/shard_map/ka,ckb->cab/dot_general | solution.py:30
  393.9 10.1 %copy.217 = f32[1,256,4096]{1,0,2:T(1,128)} copy(f32[1,256,4096]{2,1,0:T(8,128)} %mul.874) | data formatting | bytes 8388608 | tf_op jit(solution)/shard_map/mul | solution.py:80
  404.0 9.9 %maximum_bitcast_fusion = f32[2,1,256,4096]{2,0,1,3:T(2,128)} fusion(f32[1,256,4096]{1,0,2:T(1,128)} %copy.217, f32[1,256,4096]{1,0,2:T(1,128)} %copy.216), kind=kLoop, calls=%fused_computation.3 | loop fusion | flops 2097152 | bytes 16777216 | tf_op jit(solution)/shard_map/broadcast_in_dim | solution.py:108
  420.4 16.6 %fusion.396 = (f32[1024,1024]{1,0:T(8,128)}, f32[1024,1024]{1,0:T(8,128)}) fusion(f32[1024,1024]{1,0:T(8,128)} %param.7), kind=kLoop, calls=%fused_computation.412 | loop fusion | bytes 12582912 | tf_op jit(solution)/shard_map/sin | solution.py:112
  437.0 76.2 %all-to-all-done.2 = f32[2,1,256,4096]{2,0,1,3:T(2,128)} async-done(((f32[2,1,256,4096]{2,0,1,3:T(2,128)}), f32[2,1,256,4096]{2,0,1,3:T(2,128)}, u32[]{:S(2)}, u32[]{:S(2)}) %all-to-all-start.2) | async-done | bytes 8388640 | tf_op jit(solution)/shard_map/all_to_all | solution.py:107
  513.2 11.7 %fusion.394 = (f32[1,4,1,256,1024]{3,0,4,1,2:T(1,128)}, f32[1,4,1,256,1024]{3,0,4,1,2:T(1,128)}) fusion(f32[2,4,1,256,1024]{3,0,4,1,2:T(2,128)} %bitcast.38), kind=kLoop, calls=%fused_computation.410 | loop fusion | bytes 16777216 | tf_op jit(solution)/shard_map/slice | solution.py:112
  524.8 10.9 %copy.218 = f32[1,4,1,256,1024]{4,3,1,2,0:T(8,128)} copy(f32[1,4,1,256,1024]{3,0,4,1,2:T(1,128)} %get-tuple-element.19) | data formatting | bytes 8388608 | tf_op jit(solution)/shard_map/slice | solution.py:112
  535.8 11.0 %copy.219 = f32[1,4,1,256,1024]{4,3,1,2,0:T(8,128)} copy(f32[1,4,1,256,1024]{3,0,4,1,2:T(1,128)} %get-tuple-element.20) | data formatting | bytes 8388608 | tf_op jit(solution)/shard_map/slice | solution.py:112
  546.7 10.4 %fusion.1 = (f32[1024,1024]{1,0:T(8,128)S(1)}, f32[1024,1024]{1,0:T(8,128)}) fusion(f32[1024,1024]{1,0:T(8,128)} %get-tuple-element.23, f32[1,4,1,256,1024]{4,3,1,2,0:T(8,128)} %copy.219, f32[1024,1024]{1,0:T(8,128)} %get-tuple-element.24, f32[1,4,1,256,1024]{4,3,1,2,0:T(8,128)} %copy.218), kind=kLoop, calls=%fused_computation.9 | loop fusion | flops 6291456 | bytes 25165824 | tf_op jit(solution)/shard_map/sub | solution.py:40
  557.2 8.4 %fusion.11 = f32[8,128,1024]{2,0,1:T(8,128)S(1)} fusion(f32[8,128,1024]{2,1,0:T(8,128)} %bitcast.210), kind=kOutput, calls=%fused_computation.41 | convolution fusion | flops 100664192 | bytes 8388608 | tf_op jit(solution)/shard_map/ka,abc->kbc/dot_general | solution.py:30
  578.5 7.2 %multiply_subtract_fusion = (f32[8,128,1024]{2,0,1:T(8,128)S(1)}, f32[8,128,1024]{2,0,1:T(8,128)S(1)}) fusion(f32[8,128,1024]{2,0,1:T(8,128)S(1)} %fusion.83, f32[8,128]{0,1:T(8,128)S(1)} %copy.225, f32[8,128]{0,1:T(8,128)S(1)} %copy.222, f32[8,128,1024]{2,0,1:T(8,128)S(1)} %fusion.9, f32[8,128,1024]{2,1,0:T(8,128)S(1)} %bitcast.207), kind=kOutput, calls=%fused_computation.32 | convolution fusion | flops 108004224 | bytes 20979712 | tf_op jit(solution)/shard_map/ka,abc->kbc/dot_general | solution.py:30
  635.5 67.3 %collective-permute-done = f32[2,512,1024]{2,1,0:T(8,128)S(1)} collective-permute-done((f32[2,512,1024]{2,1,0:T(8,128)S(1)}, f32[2,512,1024]{2,1,0:T(8,128)S(1)}, u32[]{:S(2)}, u32[]{:S(2)}) %collective-permute-start) | collective-permute-done | bytes 4194336 | tf_op jit(solution)/shard_map/ppermute | solution.py:12
  (83 shorter events, 256.2 us)
Async XLA Ops:
  7.2 53.8 %all-to-all-start = ((f32[2,128,4096]{1,0,2:T(2,128)}), f32[2,128,4096]{1,0,2:T(2,128)}, u32[]{:S(2)}, u32[]{:S(2)}) async-start(f32[2,128,4096]{1,0,2:T(2,128)} %copy.181), calls=%async_computation | async-start | bytes 8388608 | tf_op jit(solution)/shard_map/all_to_all | solution.py:85
  119.6 6.6 copy-start.7
  119.6 6.6 copy-start.8
  140.1 98.8 %all-to-all-start.1 = ((f32[2,4,256,1024]{3,2,0,1:T(8,128)}), f32[2,4,256,1024]{3,2,0,1:T(8,128)}, u32[]{:S(2)}, u32[]{:S(2)}) async-start(f32[2,4,256,1024]{3,2,0,1:T(8,128)} %pad_maximum_fusion), calls=%async_computation.1 | async-start | bytes 16777216 | tf_op jit(solution)/shard_map/all_to_all | solution.py:95
  256.0 8.1 %copy-start.9 = (f32[1,1,256,4,1024]{4,2,0,3,1:T(8,128)S(1)}, f32[1,1,256,4,1024]{4,2,0,3,1:T(8,128)}, u32[]{:S(2)}) copy-start(f32[1,1,256,4,1024]{4,2,0,3,1:T(8,128)} %get-tuple-element.22) | copy-start | bytes 12582916
  274.3 6.3 copy-start.2
  274.3 6.3 copy-start.6
  280.6 4.0 copy-start.1
  304.9 6.9 copy-start.4
  304.9 6.9 copy-start.5
  337.2 15.5 %copy-start = (f32[256,32,128]{2,0,1:T(8,128)}, f32[256,32,128]{2,0,1:T(8,128)S(1)}, u32[]{:S(2)}) copy-start(f32[256,32,128]{2,0,1:T(8,128)S(1)} %get-tuple-element.15) | copy-start | bytes 12582916
  413.9 99.3 %all-to-all-start.2 = ((f32[2,1,256,4096]{2,0,1,3:T(2,128)}), f32[2,1,256,4096]{2,0,1,3:T(2,128)}, u32[]{:S(2)}, u32[]{:S(2)}) async-start(f32[2,1,256,4096]{2,0,1,3:T(2,128)} %maximum_bitcast_fusion), calls=%async_computation.2 | async-start | bytes 16777216 | tf_op jit(solution)/shard_map/all_to_all | solution.py:107
  557.2 8.4 %copy-start.3 = (f32[1024,1024]{1,0:T(8,128)S(1)}, f32[1024,1024]{1,0:T(8,128)}, u32[]{:S(2)}) copy-start(f32[1024,1024]{1,0:T(8,128)} %get-tuple-element.6) | copy-start | bytes 12582916
  609.0 93.8 %collective-permute-start = (f32[2,512,1024]{2,1,0:T(8,128)S(1)}, f32[2,512,1024]{2,1,0:T(8,128)S(1)}, u32[]{:S(2)}, u32[]{:S(2)}) collective-permute-start(f32[2,512,1024]{2,1,0:T(8,128)S(1)} %maximum_multiply_fusion.1), channel_id=1, source_target_pairs={{0,4},{4,8},{8,12},{1,5},{5,9},{9,13},{2,6},{6,10},{10,14},{3,7},{... | collective-permute-start | bytes 12582920 | tf_op jit(solution)/shard_map/ppermute | solution.py:12
where the time goes:
time: 718 us; the launch traced here: 706 us
  waiting for transfers between devices  236 us (33%)
  matrix products  227 us (32%)
  local copies, waits for them, and re-layouts  183 us (25%)
  other arithmetic  38.1 us (5%)
  starting transfers between devices  21.2 us (3%)
    dot_general x36, matrix products, mixing(): return jnp.einsum(spec, left, right, precision=lax.Precision.HIGHEST)  227 us
    all_to_all x1, waiting for transfers between devices, body(): lax.all_to_all(jnp.stack(filtered)[:, None], 'tile', split_axis=3, concat...  76.2 us
    ppermute x1, waiting for transfers between devices, from_behind(): return lax.ppermute(value, axis, pairs)  67.3 us
    all_to_all x1, waiting for transfers between devices, body(): lax.all_to_all(grouped, 'tile', split_axis=1, concat_axis=3, tiled=True)  60.2 us
    all_to_all x1, waiting for transfers between devices, body(): lax.all_to_all(raw_echo, 'tile', split_axis=2, concat_axis=1, tiled=True)  32 us
    slice x2, local copies, waits for them, and re-layouts, body(): returned[0]  22.6 us
    cos x2, local copies, waits for them, and re-layouts, body(): spectral = rotate(spectral, (jnp.cos(permuted), jnp.sin(permuted)))  21.9 us
    sub x2, other arithmetic, rotate(): values[0] * table[0] - values[1] * table[1]  20 us
  transfers between devices with their start and end apart: 4, of which 4 were waited for; matrix products, arithmetic and copies ran while one was open for 13% of the time, Pallas kernels for 0%

commit v1 on v0

v1 whole, which is shorter than its diff:
```python
import functools
import math

import jax
import jax.numpy as jnp
import numpy as np
from jax import lax
from jax.experimental import pallas as pl
from jax.experimental.pallas import tpu as pltpu
from jax.sharding import PartitionSpec as P

F32 = jnp.float32
BF16 = jnp.bfloat16
LANES = 128
ROW_BLOCK = 16
RADIX = 8
MEBI = 1024 * 1024
ANYWHERE = pl.BlockSpec(memory_space=pl.ANY)


def params(mebibytes=16):
    return pltpu.CompilerParams(vmem_limit_bytes=mebibytes * MEBI)


def cost():
    return pl.CostEstimate(flops=1024, bytes_accessed=1024, transcendentals=0)


def from_behind(value, axis):
    length = lax.axis_size(axis)
    return lax.ppermute(value, axis, [(i, i + 1) for i in range(length - 1)])


def exchange(value, mask):
    length = lax.axis_size("tile")
    return lax.ppermute(value, "tile", [(i, i ^ mask) for i in range(length)])


def shift(value, by):
    length = lax.axis_size("tile")
    return lax.ppermute(value, "tile", [(i, (i + by) % length) for i in range(length)])


def to_chips(pieces, arrived, last=2):
    tokens = arrived[-last] if len(arrived) >= last else []
    got = [shift(gate(piece, *tokens), 2 * k) for k, piece in enumerate(pieces) if k > 0]
    arrived.append(got)
    return [pieces[0]] + got


def gate(value, *tokens):
    return lax.optimization_barrier((value, *tokens))[0]


def split_words(value):
    high = value.astype(BF16)
    low = (value - high.astype(F32)).astype(BF16)
    return high, low


def split_table(table):
    table = table.astype(np.float32)
    high = table.astype(jnp.bfloat16)
    return high, (table - high.astype(np.float32)).astype(jnp.bfloat16)


def complex_blocks(c, s):
    return np.concatenate(
        [np.concatenate([c, -s], axis=-1), np.concatenate([s, c], axis=-1)], axis=-2
    )


def roots(residue, modulus, sign):
    angle = (residue % modulus).astype(F32) * (sign * 2.0 * math.pi / modulus)
    return jnp.cos(angle), jnp.sin(angle)


def place(offset, sizes):
    j = 0
    while offset >= sizes[j]:
        offset -= sizes[j]
        j += 1
    return offset, j


def dot(left, right):
    return jnp.dot(left, right, preferred_element_type=F32)


def times_root(value, numerator, denominator):
    re, im = value
    eighths = 8 * (numerator % denominator)
    if eighths % denominator == 0:
        octant = eighths // denominator
        half = math.sqrt(0.5)
        if octant == 0:
            return re, im
        if octant == 1:
            return (re - im) * half, (re + im) * half
        if octant == 2:
            return -im, re
        if octant == 3:
            return (re + im) * -half, (re - im) * half
        if octant == 4:
            return -re, -im
        if octant == 5:
            return (im - re) * half, (re + im) * -half
        if octant == 6:
            return im, -re
        return (re + im) * half, (im - re) * half
    angle = 2.0 * math.pi * (numerator % denominator) / denominator
    c, s = math.cos(angle), math.sin(angle)
    return re * c - im * s, re * s + im * c


def short_dft(values, sign):
    count = len(values)
    if count == 1:
        return values
    even = short_dft(values[0::2], sign)
    odd = short_dft(values[1::2], sign)
    low, high = [], []
    for k in range(count // 2):
        re, im = times_root(odd[k], sign * k, count)
        low.append((even[k][0] + re, even[k][1] + im))
        high.append((even[k][0] - re, even[k][1] - im))
    return low + high


def cos_sin(angle):
    turns = jnp.round(angle * (2.0 / math.pi))
    rest = (angle - turns * 1.57079637050628662109375) - turns * -4.37113900018624283e-8
    sq = rest * rest
    sin_r = rest + rest * sq * (-1.6666654611e-1 + sq * (8.3321608736e-3 + sq * -1.9515295891e-4))
    cos_r = 1.0 - 0.5 * sq + sq * sq * (
        4.166664568298827e-2 + sq * (-1.388731625493765e-3 + sq * 2.443315711809948e-5)
    )
    size = jnp.abs(turns)
    odd = size == 1.0
    flip = 1.0 - size
    return (
        jnp.where(odd, -turns * sin_r, flip * cos_r),
        jnp.where(odd, turns * cos_r, flip * sin_r),
    )


def turn_kernel(order_ref, phase_ref, *refs):
    cos_ref, sin_ref, column = refs[-3:]
    per = phase_ref.shape[1] // RADIX
    for lane in range(0, phase_ref.shape[2], LANES):
        column[...] = phase_ref[0, :, lane : lane + LANES]
        for a in range(RADIX):
            c, s = cos_sin(column[pl.ds(a, per, stride=RADIX), :])
            cos_ref[0, a * per : (a + 1) * per, lane : lane + LANES] = c
            sin_ref[0, a * per : (a + 1) * per, lane : lane + LANES] = s


def turns_of(phase, order, after=()):
    blocks, rows, width = phase.shape
    step = min(width, 512)
    shape = jax.ShapeDtypeStruct(phase.shape, F32)
    spec = pl.BlockSpec((1, rows, step), lambda i, j, order: (i, 0, j))
    return pl.pallas_call(
        turn_kernel,
        grid_spec=pltpu.PrefetchScalarGridSpec(
            num_scalar_prefetch=1,
            grid=(blocks, width // step),
            in_specs=[pl.BlockSpec((1, rows, step), lambda i, j, order: (order[i], 0, j))]
            + [ANYWHERE] * len(after),
            out_specs=[spec, spec],
            scratch_shapes=[pltpu.VMEM((rows, LANES), F32)],
        ),
        out_shape=[shape, shape],
        compiler_params=params(),
        cost_estimate=cost(),
        name="phase_turns",
    )(order, phase, *after)


def azimuth_front_kernel(count, place_ref, high_ref, low_ref, *refs):
    pieces, (out_ref, hi, lo) = refs[:count], refs[-3:]
    per = pieces[0].shape[1]
    half = hi.shape[0] // 2
    rows = out_ref.shape[1]
    for q in range(count):
        owner = place_ref[0] ^ q
        for part in range(2):
            top = pl.ds(pl.multiple_of(part * half + owner * per, per), per)
            hi[top, :], lo[top, :] = split_words(pieces[q][part])
    mixed = dot(high_ref[0], hi[...]) + dot(high_ref[0], lo[...]) + dot(low_ref[0], hi[...])
    out_ref[0] = mixed[:rows]
    out_ref[1] = mixed[rows:]


def azimuth_front(pieces, t, table, after=()):
    count = len(pieces)
    per, width = pieces[0].shape[1:]
    _, double, depth = table[0].shape
    step = min(width, 256)
    whole = pl.BlockSpec((1, double, depth), lambda i, t: (t[0], 0, 0))
    return pl.pallas_call(
        functools.partial(azimuth_front_kernel, count),
        grid_spec=pltpu.PrefetchScalarGridSpec(
            num_scalar_prefetch=1,
            grid=(width // step,),
            in_specs=[whole, whole]
            + [pl.BlockSpec((2, per, step), lambda i, t: (0, 0, i))] * count
            + [ANYWHERE] * len(after),
            out_specs=pl.BlockSpec((2, double // 2, step), lambda i, t: (0, 0, i)),
            scratch_shapes=[pltpu.VMEM((depth, step), BF16)] * 2,
        ),
        out_shape=jax.ShapeDtypeStruct((2, double // 2, width), F32),
        compiler_params=params(),
        cost_estimate=cost(),
        name="azimuth_front",
    )(t, *table, *pieces, *after)


def azimuth_front_table(tiles, pulses, rows, extent):
    local = np.arange(rows).reshape(rows // RADIX, RADIX).T.reshape(-1)
    doppler = np.arange(tiles)[:, None] * rows + local[None, :]
    residue = doppler[:, :, None] * np.arange(pulses) % extent
    angle = residue * (-2.0 * math.pi / extent)
    return split_table(complex_blocks(np.cos(angle), np.sin(angle)))


def sectioned_dft(load, emit, count, sign, stage_re, stage_im, rows):
    inner = min(8, count)
    outer = count // inner
    for a0 in range(outer):
        mixed = short_dft([load(outer * a1 + a0) for a1 in range(inner)], sign)
        for k in range(inner):
            re, im = times_root(mixed[k], sign * a0 * k, count)
            top = (a0 * inner + k) * rows
            stage_re[top : top + rows, :] = re
            stage_im[top : top + rows, :] = im
    for k in range(inner):
        tops = [(a0 * inner + k) * rows for a0 in range(outer)]
        mixed = short_dft(
            [(stage_re[top : top + rows, :], stage_im[top : top + rows, :]) for top in tops], sign
        )
        for m in range(outer):
            emit(k + inner * m, mixed[m])


def range_kernel(n_in, n_keep, tiles, widths, place_ref, *refs):
    refs = list(refs)
    u_refs = [refs.pop(0) for _ in range(n_in)]
    cs_ref, ss_ref, cr_ref, sr_ref, front_ref, back_ref, wf_ref, wi_ref = [
        refs.pop(0) for _ in range(8)
    ]
    del refs[:n_keep]
    outs = [[refs.pop(0) for _ in range(tiles // 2)] for _ in widths]
    core = place_ref[0] % 2
    stage_re, stage_im, hi, lo, mid = refs
    rows = stage_re.shape[0] * LANES // (cr_ref.shape[2])
    count = cr_ref.shape[2] // LANES
    per_tile = cs_ref.shape[2] // LANES

    def load(a):
        lane, j = place(a * LANES, [u.shape[2] for u in u_refs])
        u = u_refs[j]
        re, im = u[0, :, lane : lane + LANES], u[1, :, lane : lane + LANES]
        lane = (a % per_tile) * LANES
        c = cs_ref[a // per_tile, :, lane : lane + LANES]
        s = ss_ref[a // per_tile, :, lane : lane + LANES]
        return re * c - im * s, re * s + im * c

    def put(k, re, im):
        top = k * rows
        hi[top : top + rows, :LANES], lo[top : top + rows, :LANES] = split_words(re)
        hi[top : top + rows, LANES:], lo[top : top + rows, LANES:] = split_words(im)

    def emit_front(k, value):
        re, im = value
        c, s = front_ref[0, k : k + 1, :], front_ref[1, k : k + 1, :]
        put(k, re * c - im * s, re * s + im * c)

    sectioned_dft(load, emit_front, count, -1, stage_re, stage_im, rows)
    high = hi[...]
    mid[...] = dot(jnp.concatenate([high, lo[...], high], axis=1), wf_ref[...])
    for k in range(count):
        top = k * rows
        re, im = mid[top : top + rows, :LANES], mid[top : top + rows, LANES:]
        c = cr_ref[0, :, k * LANES : (k + 1) * LANES]
        s = sr_ref[0, :, k * LANES : (k + 1) * LANES]
        put(k, re * c - im * s, re * s + im * c)
    high = hi[...]
    mid[...] = dot(jnp.concatenate([high, lo[...], high], axis=1), wi_ref[...])

    def load_back(k):
        top = k * rows
        re, im = mid[top : top + rows, :LANES], mid[top : top + rows, LANES:]
        c, s = back_ref[0, k : k + 1, :], back_ref[1, k : k + 1, :]
        return re * c - im * s, re * s + im * c

    def emit_back(a, value):
        lane, j = place((a % per_tile) * LANES, widths)
        tile = a // per_tile
        out, toward = outs[j][tile // 2], (tile % 2) ^ core
        out[toward, 0, :, lane : lane + LANES] = value[0]
        out[toward, 1, :, lane : lane + LANES] = value[1]

    sectioned_dft(load_back, emit_back, count, 1, stage_re, stage_im, rows)


def range_tables(t, tiles, count):
    k = jnp.arange(count, dtype=jnp.int32)[:, None]
    b = jnp.arange(LANES, dtype=jnp.int32)[None, :]
    extent = count * LANES
    front = jnp.stack(roots(k * b, extent, -1.0))
    back = jnp.stack(roots(k * (b + t // 2 * 2 * (extent // tiles)), extent, 1.0)) * (1.0 / extent)
    return front, back


def range_mix(sign):
    index = np.arange(LANES)
    angle = (index[:, None] * index[None, :] % LANES) * (sign * 2.0 * math.pi / LANES)
    c, s = np.cos(angle), np.sin(angle)
    table = np.block([[c, s], [-s, c]]).astype(np.float32)
    high = table.astype(jnp.bfloat16)
    low = (table - high.astype(np.float32)).astype(jnp.bfloat16)
    return jnp.asarray(np.concatenate([high, high, low], axis=0))


def range_pass(spectra, t, scaling, ranging, front, back, span, split, widths, earlier, after):
    rows = spectra[0].shape[1]
    tiles, _, width = scaling[0].shape
    extent = ranging[0].shape[2]
    count = extent // LANES
    block = ROW_BLOCK
    first, steps = span
    wf, wi = range_mix(-1.0), range_mix(1.0)
    in_specs = [
        pl.BlockSpec((2, block, u.shape[2]), lambda i, t: (0, first + i, 0)) for u in spectra
    ]
    in_specs += [pl.BlockSpec((tiles, block, width), lambda i, t: (0, first + i, 0))] * 2
    in_specs += [pl.BlockSpec((1, block, extent), lambda i, t: (0, first + i, 0))] * 2
    in_specs += [pl.BlockSpec((2, count, LANES), lambda i, t: (0, 0, 0))] * 2
    in_specs += [pl.BlockSpec(wf.shape, lambda i, t: (0, 0))] * 2
    n_base = 1 + len(in_specs)
    in_specs += [ANYWHERE] * (len(earlier) + len(after))
    chips = tiles // 2
    out_specs, out_shape = [], []
    for j, out_width in enumerate(widths):
        lead = 0 if j < split else first
        out_rows = steps * block if j < split else rows
        spec = pl.BlockSpec(
            (2, 2, block, out_width), lambda i, t, lead=lead: (0, 0, lead + i, 0)
        )
        out_specs += [spec] * chips
        out_shape += [jax.ShapeDtypeStruct((2, 2, out_rows, out_width), F32)] * chips
    aliases = {n_base + i: split * chips + i for i in range(len(earlier))}
    flat = pl.pallas_call(
        functools.partial(range_kernel, len(spectra), len(earlier) + len(after), tiles, widths),
        grid_spec=pltpu.PrefetchScalarGridSpec(
            num_scalar_prefetch=1,
            grid=(steps,),
            in_specs=in_specs,
            out_specs=out_specs,
            scratch_shapes=[
                pltpu.VMEM((count * block, LANES), F32),
                pltpu.VMEM((count * block, LANES), F32),
                pltpu.VMEM((count * block, 2 * LANES), BF16),
                pltpu.VMEM((count * block, 2 * LANES), BF16),
                pltpu.VMEM((count * block, 2 * LANES), F32),
            ],
        ),
        out_shape=out_shape,
        input_output_aliases=aliases,
        compiler_params=params(),
        cost_estimate=cost(),
        name="range_filter",
    )(t, *spectra, *scaling, *ranging, front, back, wf, wi, *earlier, *after)
    return [flat[j * chips : (j + 1) * chips] for j in range(len(widths))]


def azimuth_back_kernel(layout, place_ref, high_ref, low_ref, cos_ref, sin_ref, *refs):
    total = sum(len(rows) for rows in layout)
    pieces, (head_ref, tail_ref, kbuf, z) = refs[:total], refs[-4:]
    grouped, at = [], 0
    for rows in layout:
        grouped.append(list(zip(rows, pieces[at : at + len(rows)])))
        at += len(rows)
    per = cos_ref.shape[1] // RADIX
    mixed_rows = z.shape[1] // 2
    tiles = len(layout)
    for a in range(RADIX):
        for r, group in enumerate(grouped):
            owner = lax.rem(place_ref[0] + tiles - r // 2 * 2, tiles) ^ (r % 2)
            first, low = 0, a * per
            for rows, piece in group:
                high = min((a + 1) * per, first + rows)
                if first <= low < high:
                    c, s = cos_ref[owner, low:high, :], sin_ref[owner, low:high, :]
                    re = piece[0, 0, low - first : high - first, :]
                    im = piece[0, 1, low - first : high - first, :]
                    top = pl.ds(pl.multiple_of(owner * per + low - a * per, 8), high - low)
                    kbuf[0, top, :] = re * c - im * s
                    kbuf[1, top, :] = re * s + im * c
                    low = high
                first += rows
        hi, lo = split_words(kbuf[...].reshape(z.shape[1:]))
        z[a] = dot(high_ref[a], hi) + dot(high_ref[a], lo) + dot(low_ref[a], hi)
    half = RADIX // 2
    for low in range(0, mixed_rows, 8):
        values = [
            (z[a, low : low + 8, :], z[a, mixed_rows + low : mixed_rows + low + 8, :])
            for a in range(RADIX)
        ]
        for p, value in enumerate(short_dft(values, 1)):
            ref = head_ref if p < half else tail_ref
            top = (p % half) * mixed_rows + low
            ref[0, top : top + 8, :] = value[0]
            ref[1, top : top + 8, :] = value[1]


def azimuth_back(pieces, t, turns, table, column, after=()):
    flat = [piece for group in pieces for piece in group]
    layout = [[piece.shape[2] for piece in group] for group in pieces]
    width = flat[0].shape[3]
    tiles, rows, _ = turns[0].shape
    double = table[0].shape[1]
    out_rows = RADIX * double // 4
    out = jax.ShapeDtypeStruct((2, out_rows, width), F32)
    whole = pl.BlockSpec(table[0].shape, lambda i, t: (0, 0, 0))
    turn = pl.BlockSpec((tiles, rows, width), lambda i, t: (0, 0, column // width))
    return pl.pallas_call(
        functools.partial(azimuth_back_kernel, layout),
        grid_spec=pltpu.PrefetchScalarGridSpec(
            num_scalar_prefetch=1,
            grid=(1,),
            in_specs=[whole, whole, turn, turn]
            + [pl.BlockSpec((1, *piece.shape[1:]), lambda i, t: (0, 0, 0, 0)) for piece in flat]
            + [ANYWHERE] * len(after),
            out_specs=[pl.BlockSpec((2, out_rows, width), lambda i, t: (0, 0, 0))] * 2,
            scratch_shapes=[
                pltpu.VMEM((2, double // 2, width), F32),
                pltpu.VMEM((RADIX, double, width), F32),
            ],
        ),
        out_shape=[out, out],
        compiler_params=params(24),
        cost_estimate=cost(),
        name="azimuth_back",
    )(t, *table, *turns, *flat, *after)


def azimuth_back_table(extent):
    index = np.arange(extent // RADIX)
    doppler = RADIX * index[None, :] + np.arange(RADIX)[:, None]
    residue = doppler[:, None, :] * index[None, :, None] % extent
    angle = residue * (2.0 * math.pi / extent)
    return split_table(complex_blocks(np.cos(angle), np.sin(angle)) / extent)


def add_kernel(head_ref, tail_ref, *refs):
    refs[-1][...] = head_ref[...] + tail_ref[...]


def add_tail(head, tail, earlier, column, full_width):
    _, rows, width = head.shape
    spec = pl.BlockSpec((1, rows, width), lambda i: (i, 0, 0))
    kept = [] if earlier is None else [earlier]
    return pl.pallas_call(
        add_kernel,
        grid=(2,),
        in_specs=[spec, spec] + [ANYWHERE] * len(kept),
        out_specs=pl.BlockSpec((1, rows, width), lambda i: (i, 0, column // width)),
        out_shape=jax.ShapeDtypeStruct((2, rows, full_width), F32),
        input_output_aliases={2: 0} if kept else {},
        compiler_params=params(),
        cost_estimate=cost(),
        name="add_tail",
    )(head, tail, *kept)


def scaling_cuts(phase_scaling, rows):
    tiles = lax.axis_size("tile")
    t = lax.axis_index("tile")
    copies = lax.axis_size("strip") * lax.axis_size("az")
    replica = lax.axis_index("strip") * lax.axis_size("az") + lax.axis_index("az")
    share = rows // copies

    def rows_at(start, size):
        return lax.dynamic_slice(phase_scaling, (start, 0), (size, phase_scaling.shape[1]))

    near = [rows_at((t ^ q) * rows, rows) for q in range(2)]
    far = [rows_at((t ^ q) * rows + replica * share, share) for q in range(2, tiles)]
    return near, far


def body(raw_echo, phase_scaling, phase_range, phase_azimuth):
    tiles = lax.axis_size("tile")
    t = lax.axis_index("tile")
    place_t = t.reshape(1)
    per, ranges = raw_echo.shape[1:]
    extent, width = phase_scaling.shape
    rows = phase_range.shape[0]
    count = ranges // LANES
    index = jnp.arange(tiles, dtype=jnp.int32)

    near, far = scaling_cuts(phase_scaling, rows)
    far_sent = [exchange(cut, q + 2) for q, cut in enumerate(far)]

    eighth = ranges // 8
    straight, at = [], 0
    for size in (4 * eighth, 3 * eighth, eighth):
        piece = gate(raw_echo[:, :, at : at + size], *far_sent)
        at += size
        straight.append([piece] + [exchange(piece, q) for q in range(2, tiles, 2)])

    far_all = lax.all_gather(jnp.stack(far_sent), ("strip", "az"))
    near[1] = exchange(near[1], 1)

    permuted = phase_range.reshape(rows, LANES, count).transpose(0, 2, 1).reshape(1, rows, ranges)
    ranging = turns_of(permuted, jnp.zeros((1,), jnp.int32))
    azimuth = turns_of(phase_azimuth.reshape(tiles, rows, width), index, after=[ranging[0]])
    front, back = range_tables(t, tiles, count)
    front_table = azimuth_front_table(tiles, per * tiles, rows, extent)
    back_table = azimuth_back_table(extent)

    tokens = [azimuth[0], front, back]
    spectra = []
    for j, received in enumerate(straight):
        received = [gate(piece, *tokens) for piece in received]
        handed = [exchange(piece, 1) for piece in received]
        got = [piece for pair in zip(received, handed) for piece in pair]
        spectra.append(azimuth_front(got, place_t, front_table))
        tokens = [spectra[-1]]
        if j == 0:
            far_rows = gate(far_all, *tokens).transpose(1, 0, 2, 3)
            far_rows = far_rows.reshape(tiles - 2, rows, width)
            pieces = jnp.concatenate([near[0][None], near[1][None], far_rows])
            scaling = turns_of(pieces, t ^ index)
            tokens = [scaling[0]]

    if width >= 8 * LANES:
        widths = [width // 4] * 3 + [width // 8] * 2
    else:
        widths = [LANES] * (width // LANES)
    blocks = rows // ROW_BLOCK
    spans = [(0, blocks)] if blocks < 16 else [(0, blocks // 2), (blocks // 2, blocks // 2)]
    split = 1 if len(spans) > 1 else 0
    parts, kept, sequence = [], [], []
    for span in spans:
        done = range_pass(
            spectra, place_t, scaling, ranging, front, back, span, split, widths, kept, []
        )
        parts.append([to_chips(chunk, sequence, 1) for chunk in done[:split]])
        kept = [piece for chunk in done[split:] for piece in chunk]
    arrived = [[part[j] for part in parts] for j in range(split)]
    for j, chunk in enumerate(done[split:]):
        arrived.append([to_chips(chunk, sequence, 1 if j == 0 else 2)])

    heads, tails, images, column = [], [], [], 0
    for j, groups in enumerate(arrived):
        groups = [[gate(piece, *heads[-1:]) for piece in group] for group in groups]
        pieces = []
        for k in range(tiles // 2):
            pieces.append([group[k] for group in groups])
            pieces.append([exchange(group[k][1:], 1) for group in groups])
        before = heads[-1:]
        head, tail = azimuth_back(pieces, place_t, azimuth, back_table, column, after=before)
        heads.append(head)
        tokens = [tails[-1][0]] if tails else []
        tails.append((from_behind(gate(tail, *tokens), "az"), column))
        column += widths[j]
        if j >= 2:
            tail, at = tails[j - 2]
            image = images[-1] if images else None
            images.append(add_tail(heads[j - 2], tail, image, at, width))
    for j in range(len(images), len(heads)):
        tail, at = tails[j]
        images.append(add_tail(heads[j], tail, images[-1] if images else None, at, width))
    return images[-1]


def solution(mesh):
    return jax.shard_map(
        body,
        mesh=mesh,
        in_specs=(
            P(None, ("strip", "az", "tile"), None),
            P(None, "tile"),
            P("tile", None),
            P(None, "tile"),
        ),
        out_specs=P(None, ("strip", "az"), "tile"),
        check_vma=False,
    )
```

time: 718 us -> 287 us (0.40); the launches traced: 706 us -> 286 us
  matrix products: 227 us -> 0 us
  local copies, waits for them, and re-layouts: 183 us -> 46.9 us
  waiting for transfers between devices: 236 us -> 104 us
  Pallas kernels: 0 us -> 78.1 us
  other arithmetic: 38.1 us -> 2.74 us
  starting transfers between devices: 21.2 us -> 40.5 us
  between operations: 0.89 us -> 14 us
    dot_general x36 -> x0, matrix products: 227 us -> none  [mixing(): return jnp.einsum(spec, left, right, precision=lax.Precision.HIGHEST)]
    all_to_all x3 -> x0, waiting for transfers between devices: 168 us -> none  [the longest x1 76.2 us: body(): lax.all_to_all(jnp.stack(filtered)[:, None], 'tile', split_axis=3, concat...]
    pallas_call x0 -> x18, Pallas kernels: none -> 78.1 us  [the longest x2 24.8 us: range_pass(): pl.pallas_call(functools.partial(range_kernel, len(spectra), len(earlier)...]
    slice x7 -> x15, local copies, waits for them, and re-layouts: 53 us -> 5.75 us  [the longest x3 5.46 us: body(): piece = gate(raw_echo[:, :, at:at + size], *far_sent)]
    sin x5 -> x0, local copies, waits for them, and re-layouts: 38.7 us -> none  [the longest x1 16.6 us: body(): jnp.sin(phase_scaling)]
    ppermute x1 -> x35, waiting for transfers between devices: 67.3 us -> 104 us  [the longest x6 53.1 us: shift(): lax.ppermute(value, 'tile', [(i, (i + by) % length) for i in range(length)])]
    ppermute x1 -> x35, starting transfers between devices: 4.51 us -> 40.5 us  [the longest x5 21.4 us: from_behind(): return lax.ppermute(value, axis, [(i, i + 1) for i in range(length - 1)])]
    mul x4 -> x0, local copies, waits for them, and re-layouts: 30.5 us -> none  [the longest x2 15.4 us: range_inverse(): mixed[0].reshape(width, extent) * scale]
  transfers between devices with their start and end apart: 4 -> 36, of which waited for: 4 -> 28; matrix products, arithmetic and copies ran while one was open for 13% -> 10% of each run, Pallas kernels for 0% -> 22%
where the time goes in v1:
time: 287 us; the launch traced here: 286 us
  waiting for transfers between devices  104 us (36%)
  Pallas kernels  78.1 us (27%)
  local copies, waits for them, and re-layouts  46.9 us (16%)
  starting transfers between devices  40.5 us (14%)
  between operations  14 us (5%)
    ppermute x6, waiting for transfers between devices, shift(): lax.ppermute(value, 'tile', [(i, (i + by) % length) for i in range(length)])  53.1 us
    ppermute x24, waiting for transfers between devices, exchange(): return lax.ppermute(value, 'tile', [(i, i ^ mask) for i in range(length)])  30.2 us
    pallas_call x2, Pallas kernels, range_pass(): pl.pallas_call(functools.partial(range_kernel, len(spectra), len(earlier)...  24.8 us
    unnamed x49, local copies, waits for them, and re-layouts  24.5 us
    pallas_call x3, Pallas kernels, azimuth_front(): pl.pallas_call(functools.partial(azimuth_front_kernel, count), grid_spec=...  21.5 us
    ppermute x5, starting transfers between devices, from_behind(): return lax.ppermute(value, axis, [(i, i + 1) for i in range(length - 1)])  21.4 us
    ppermute x5, waiting for transfers between devices, from_behind(): return lax.ppermute(value, axis, [(i, i + 1) for i in range(length - 1)])  20.7 us
    pallas_call x3, Pallas kernels, turns_of(): pl.pallas_call(turn_kernel, grid_spec=pltpu.PrefetchScalarGridSpec(num_sc...  19.9 us
  transfers between devices with their start and end apart: 36, of which 28 were waited for; matrix products, arithmetic and copies ran while one was open for 10% of the time, Pallas kernels for 22%

profile of v1, /device:TPU:0, one launch (start us, length us, event | category | flops | bytes accessed | tf_op | source)
XLA Modules:
  0.0 286.2 jit_solution(15408127969563466369)
XLA Ops:
  19.9 5.6 %copy.30 = f32[256,4096]{0,1:T(8,128)} copy(f32[256,4096]{1,0:T(8,128)} %param.14) | data formatting | bytes 8388608 | tf_op args[2]
  25.5 6.0 %copy.31 = f32[256,32,128]{2,1,0:T(8,128)} copy(f32[256,32,128]{0,1,2:T(8,128)} %bitcast.15) | data formatting | bytes 8388608 | tf_op jit(solution)/shard_map/transpose | solution.py:516
  31.5 4.9 %reshape.190.phase_ref = f32[1,256,4096]{2,1,0:T(8,128)} reshape(f32[256,32,128]{2,1,0:T(8,128)} %copy.31) | data formatting | bytes 8388608 | tf_op jit(solution)/shard_map/reshape | solution.py:516
  38.7 6.2 %phase_turns.3 = (f32[1,256,4096]{2,1,0:T(8,128)S(1)}, f32[1,256,4096]{2,1,0:T(8,128)S(1)}) custom-call(s32[1]{0:T(128)} %constant.62.clone.1.order_ref, f32[1,256,4096]{2,1,0:T(8,128)S(1)} %copy-done.20), custom_call_target="tpu_custom_call" | custom-call | flops 1024 | bytes 1024 | tf_op jit(solution)/shard_map/phase_turns/pallas_call | solution.py:163
  46.9 6.8 %phase_turns.4 = (f32[4,256,1024]{2,1,0:T(8,128)S(1)}, f32[4,256,1024]{2,1,0:T(8,128)S(1)}) custom-call(s32[4]{0:T(128)S(1)} %iota.34.order_ref, f32[4,256,1024]{2,1,0:T(8,128)S(1)} %bitcast.14, f32[1,256,4096]{2,1,0:T(8,128)S(1)} %get-tuple-element.68.refs_0_.refs_5_), custom_call_target="tpu_custom_call" | custom-call | flops 1024 | bytes 1024 | tf_op jit(solution)/shard_map/phase_turns/pallas_call | solution.py:163
  60.1 5.0 %collective-permute-done.3.refs_2_ = f32[2,128,2048]{2,1,0:T(8,128)} collective-permute-done((f32[2,128,2048]{2,1,0:T(8,128)S(1)}, f32[2,128,2048]{2,1,0:T(8,128)}, u32[]{:S(2)}, u32[]{:S(2)}) %collective-permute-start.3) | collective-permute-done | bytes 2097184 | tf_op jit(solution)/shard_map/ppermute | solution.py:36
  74.9 10.7 %azimuth_front.3.refs_0_ = f32[2,256,2048]{2,1,0:T(8,128)S(1)} custom-call(s32[1]{0:T(128)} %bitcast.place_ref, bf16[4,512,1024]{2,1,0:T(8,128)(2,1)S(1)} %copy-done.6, bf16[4,512,1024]{2,1,0:T(8,128)(2,1)S(1)} %copy-done.4, f32[2,128,2048]{2,1,0:T(8,128)S(1)} %slice.45.refs_0_, f32[2,128,2048]{2,1,0:T(8,128)} %collective-permute-done.2.refs_1_, ...), custom_call_target="tpu_custom_call" | custom-call | flops 1024 | bytes 1024 | tf_op jit(solution)/shard_map/azimuth_front/pallas_call | solution.py:201
  91.2 6.8 %phase_turns.5 = (f32[4,256,1024]{2,1,0:T(8,128)S(1)}, f32[4,256,1024]{2,1,0:T(8,128)S(1)}) custom-call(s32[4]{0:T(128)S(1)} %iota_xor_fusion.order_ref, f32[4,256,1024]{2,1,0:T(8,128)S(1)} %pad_maximum_fusion.phase_ref), custom_call_target="tpu_custom_call" | custom-call | flops 1024 | bytes 1024 | tf_op jit(solution)/shard_map/phase_turns/pallas_call | solution.py:163
  98.1 6.9 %collective-permute-done.7.refs_2_ = f32[2,128,1536]{2,1,0:T(8,128)} collective-permute-done((f32[2,128,1536]{2,1,0:T(8,128)}, f32[2,128,1536]{2,1,0:T(8,128)}, u32[]{:S(2)}, u32[]{:S(2)}) %collective-permute-start.7) | collective-permute-done | bytes 1572896 | tf_op jit(solution)/shard_map/ppermute | solution.py:36
  110.8 8.3 %azimuth_front.4.refs_1_ = f32[2,256,1536]{2,1,0:T(8,128)S(1)} custom-call(s32[1]{0:T(128)} %bitcast.place_ref, bf16[4,512,1024]{2,1,0:T(8,128)(2,1)S(1)} %copy-done.7, bf16[4,512,1024]{2,1,0:T(8,128)(2,1)S(1)} %copy-done.5, f32[2,128,1536]{2,1,0:T(8,128)} %slice.46.refs_0_, f32[2,128,1536]{2,1,0:T(8,128)S(1)} %collective-permute-done.6.refs_1_, ...), custom_call_target="tpu_custom_call" | custom-call | flops 1024 | bytes 1024 | tf_op jit(solution)/shard_map/azimuth_front/pallas_call | solution.py:201
  125.7 12.3 %range_filter.2 = (f32[2,2,128,256]{3,2,1,0:T(8,128)S(1)}, f32[2,2,128,256]{3,2,1,0:T(8,128)S(1)}, f32[2,2,256,256]{3,2,1,0:T(8,128)S(1)}, f32[2,2,256,256]{3,2,...) custom-call(s32[1]{0:T(128)} %bitcast.place_ref, ...), custom_call_target="tpu_custom_call" | custom-call | flops 1024 | bytes 1024 | tf_op jit(solution)/shard_map/range_filter/pallas_call | solution.py:354
  144.2 12.5 %range_filter.3 = (f32[2,2,128,256]{3,2,1,0:T(8,128)S(1)}, f32[2,2,128,256]{3,2,1,0:T(8,128)S(1)}, f32[2,2,256,256]{3,2,1,0:T(8,128)S(1)}, f32[2,2,256,256]{3,2,...) custom-call(s32[1]{0:T(128)} %bitcast.place_ref, ...), custom_call_target="tpu_custom_call", output_to_operand_aliasing={{2}: (12, {}), {3}: (13, {}), {4}: (14, {}), {5}: (15, {}),... | custom-call | flops 1024 | bytes 1024 | tf_op jit(solution)/shard_map/range_filter/pallas_call | solution.py:354
  157.0 13.4 %collective-permute-done.15.refs_5_ = f32[2,2,128,256]{3,2,1,0:T(8,128)S(1)} collective-permute-done((f32[2,2,128,256]{3,2,1,0:T(8,128)S(1)}, f32[2,2,128,256]{3,2,1,0:T(8,128)S(1)}, u32[]{:S(2)}, u32[]{:S(2)}) %collective-permute-start.15) | collective-permute-done | bytes 524320 | tf_op jit(solution)/shard_map/ppermute | solution.py:41
  175.1 3.7 %collective-permute-start.30 = (f32[2,512,256]{2,1,0:T(8,128)S(1)}, f32[2,512,256]{2,1,0:T(8,128)S(1)}, u32[]{:S(2)}, u32[]{:S(2)}) collective-permute-start(f32[2,512,256]{2,1,0:T(8,128)S(1)} %get-tuple-element.126), channel_id=1, source_target_pairs={{0,4},{4,8},{8,12},{1,5},{5,9},{9,13},{2,6},{6,10},{10,14},{3,7},{... | collective-permute-start | bytes 3145736 | tf_op jit(solution)/shard_map/ppermute | solution.py:31
  180.6 15.9 %collective-permute-done.19.refs_2_ = f32[2,2,256,256]{3,2,1,0:T(8,128)S(1)} collective-permute-done((f32[2,2,256,256]{3,2,1,0:T(8,128)S(1)}, f32[2,2,256,256]{3,2,1,0:T(8,128)S(1)}, u32[]{:S(2)}, u32[]{:S(2)}) %collective-permute-start.19) | collective-permute-done | bytes 1048608 | tf_op jit(solution)/shard_map/ppermute | solution.py:41
  201.5 4.4 %collective-permute-start.31 = (f32[2,512,256]{2,1,0:T(8,128)S(1)}, f32[2,512,256]{2,1,0:T(8,128)S(1)}, u32[]{:S(2)}, u32[]{:S(2)}) collective-permute-start(f32[2,512,256]{2,1,0:T(8,128)S(1)} %get-tuple-element.127), channel_id=1, source_target_pairs={{0,4},{4,8},{8,12},{1,5},{5,9},{9,13},{2,6},{6,10},{10,14},{3,7},{... | collective-permute-start | bytes 3145736 | tf_op jit(solution)/shard_map/ppermute | solution.py:31
  206.0 10.9 %collective-permute-done.22.refs_2_ = f32[2,2,256,256]{3,2,1,0:T(8,128)S(1)} collective-permute-done((f32[2,2,256,256]{3,2,1,0:T(8,128)S(1)}, f32[2,2,256,256]{3,2,1,0:T(8,128)S(1)}, u32[]{:S(2)}, u32[]{:S(2)}) %collective-permute-start.22) | collective-permute-done | bytes 1048608 | tf_op jit(solution)/shard_map/ppermute | solution.py:41
  220.6 7.2 %collective-permute-done.31.tail_ref = f32[2,512,256]{2,1,0:T(8,128)S(1)} collective-permute-done((f32[2,512,256]{2,1,0:T(8,128)S(1)}, f32[2,512,256]{2,1,0:T(8,128)S(1)}, u32[]{:S(2)}, u32[]{:S(2)}) %collective-permute-start.31) | collective-permute-done | bytes 1048608 | tf_op jit(solution)/shard_map/ppermute | solution.py:31
  227.7 4.4 %collective-permute-start.32 = (f32[2,512,256]{2,1,0:T(8,128)S(1)}, f32[2,512,256]{2,1,0:T(8,128)S(1)}, u32[]{:S(2)}, u32[]{:S(2)}) collective-permute-start(f32[2,512,256]{2,1,0:T(8,128)S(1)} %get-tuple-element.128), channel_id=1, source_target_pairs={{0,4},{4,8},{8,12},{1,5},{5,9},{9,13},{2,6},{6,10},{10,14},{3,7},{... | collective-permute-start | bytes 3145736 | tf_op jit(solution)/shard_map/ppermute | solution.py:31
  234.3 12.8 %collective-permute-done.25.refs_2_ = f32[2,2,256,128]{3,2,1,0:T(8,128)S(1)} collective-permute-done((f32[2,2,256,128]{3,2,1,0:T(8,128)S(1)}, f32[2,2,256,128]{3,2,1,0:T(8,128)S(1)}, u32[]{:S(2)}, u32[]{:S(2)}) %collective-permute-start.25) | collective-permute-done | bytes 524320 | tf_op jit(solution)/shard_map/ppermute | solution.py:41
  253.1 4.4 %collective-permute-start.33 = (f32[2,512,128]{2,1,0:T(8,128)S(1)}, f32[2,512,128]{2,1,0:T(8,128)S(1)}, u32[]{:S(2)}, u32[]{:S(2)}) collective-permute-start(f32[2,512,128]{2,1,0:T(8,128)S(1)} %get-tuple-element.129), channel_id=1, source_target_pairs={{0,4},{4,8},{8,12},{1,5},{5,9},{9,13},{2,6},{6,10},{10,14},{3,7},{... | collective-permute-start | bytes 1572872 | tf_op jit(solution)/shard_map/ppermute | solution.py:31
  260.7 5.5 %collective-permute-done.33.tail_ref = f32[2,512,128]{2,1,0:T(8,128)S(1)} collective-permute-done((f32[2,512,128]{2,1,0:T(8,128)S(1)}, f32[2,512,128]{2,1,0:T(8,128)S(1)}, u32[]{:S(2)}, u32[]{:S(2)}) %collective-permute-start.33) | collective-permute-done | bytes 524320 | tf_op jit(solution)/shard_map/ppermute | solution.py:31
  266.2 4.4 %collective-permute-start.34 = (f32[2,512,128]{2,1,0:T(8,128)S(1)}, f32[2,512,128]{2,1,0:T(8,128)S(1)}, u32[]{:S(2)}, u32[]{:S(2)}) collective-permute-start(f32[2,512,128]{2,1,0:T(8,128)S(1)} %get-tuple-element.130), channel_id=1, source_target_pairs={{0,4},{4,8},{8,12},{1,5},{5,9},{9,13},{2,6},{6,10},{10,14},{3,7},{... | collective-permute-start | bytes 1572872 | tf_op jit(solution)/shard_map/ppermute | solution.py:31
  274.6 3.9 %collective-permute-done.34.tail_ref = f32[2,512,128]{2,1,0:T(8,128)S(1)} collective-permute-done((f32[2,512,128]{2,1,0:T(8,128)S(1)}, f32[2,512,128]{2,1,0:T(8,128)S(1)}, u32[]{:S(2)}, u32[]{:S(2)}) %collective-permute-start.34) | collective-permute-done | bytes 524320 | tf_op jit(solution)/shard_map/ppermute | solution.py:31
  (145 shorter events, 89.0 us)
Async XLA Ops:
  6.5 81.0 %all-gather.3.cloned.1.call-start = ((), (), s32[]{:S(2)}) async-start(), calls=%async_computation | async-start | bytes 2359296 | tf_op jit(solution)/shard_map/all_gather | solution.py:513
  7.5 6.4 %collective-permute-start.1 = (f32[32,1024]{1,0:T(8,128)S(1)}, f32[32,1024]{1,0:T(8,128)S(1)}, u32[]{:S(2)}, u32[]{:S(2)}) collective-permute-start(f32[32,1024]{1,0:T(8,128)S(1)} %get-tuple-element.133), channel_id=1, source_target_pairs={{0,3},{1,2},{2,1},{3,0},{4,7},{5,6},{6,5},{7,4},{8,11},{9,10},{10,... | collective-permute-start | bytes 393224 | tf_op jit(solution)/shard_map/ppermute | solution.py:36
  10.0 6.9 %collective-permute-start = (f32[32,1024]{1,0:T(8,128)S(1)}, f32[32,1024]{1,0:T(8,128)S(1)}, u32[]{:S(2)}, u32[]{:S(2)}) collective-permute-start(f32[32,1024]{1,0:T(8,128)S(1)} %get-tuple-element.134), channel_id=1, source_target_pairs={{0,2},{1,3},{2,0},{3,1},{4,6},{5,7},{6,4},{7,5},{8,10},{9,11},{10,... | collective-permute-start | bytes 393224 | tf_op jit(solution)/shard_map/ppermute | solution.py:36
  16.9 48.3 %collective-permute-start.3 = (f32[2,128,2048]{2,1,0:T(8,128)S(1)}, f32[2,128,2048]{2,1,0:T(8,128)}, u32[]{:S(2)}, u32[]{:S(2)}) collective-permute-start(f32[2,128,2048]{2,1,0:T(8,128)S(1)} %slice.45.refs_0_), channel_id=1, source_target_pairs={{0,2},{1,3},{2,0},{3,1},{4,6},{5,7},{6,4},{7,5},{8,10},{9,11},{10,... | collective-permute-start | bytes 6291464 | tf_op jit(solution)/shard_map/ppermute | solution.py:36
  60.1 12.6 %collective-permute-start.2 = (f32[2,128,2048]{2,1,0:T(8,128)S(1)}, f32[2,128,2048]{2,1,0:T(8,128)}, u32[]{:S(2)}, u32[]{:S(2)}) collective-permute-start(f32[2,128,2048]{2,1,0:T(8,128)S(1)} %slice.45.refs_0_), channel_id=1, source_target_pairs={{0,1},{1,0},{2,3},{3,2},{4,5},{5,4},{6,7},{7,6},{8,9},{9,8},{10,11... | collective-permute-start | bytes 6291464 | tf_op jit(solution)/shard_map/ppermute | solution.py:36
  65.2 7.5 %collective-permute-start.4 = (f32[2,128,2048]{2,1,0:T(8,128)}, f32[2,128,2048]{2,1,0:T(8,128)}, u32[]{:S(2)}, u32[]{:S(2)}) collective-permute-start(f32[2,128,2048]{2,1,0:T(8,128)} %collective-permute-done.3.refs_2_), channel_id=1, source_target_pairs={{0,1},{1,0},{2,3},{3,2},{4,5},{5,4},{6,7},{7,6},{8,9},{9,8},{10,11... | collective-permute-start | bytes 6291464 | tf_op jit(solution)/shard_map/ppermute | solution.py:36
  67.8 37.1 %collective-permute-start.7 = (f32[2,128,1536]{2,1,0:T(8,128)}, f32[2,128,1536]{2,1,0:T(8,128)}, u32[]{:S(2)}, u32[]{:S(2)}) collective-permute-start(f32[2,128,1536]{2,1,0:T(8,128)} %slice.46.refs_0_), channel_id=1, source_target_pairs={{0,2},{1,3},{2,0},{3,1},{4,6},{5,7},{6,4},{7,5},{8,10},{9,11},{10,... | collective-permute-start | bytes 4718600 | tf_op jit(solution)/shard_map/ppermute | solution.py:36
  72.4 16.9 %collective-permute-start.5 = (f32[256,1024]{1,0:T(8,128)}, f32[256,1024]{1,0:T(8,128)}, u32[]{:S(2)}, u32[]{:S(2)}) collective-permute-start(f32[256,1024]{1,0:T(8,128)} %get-tuple-element.132), channel_id=1, source_target_pairs={{0,1},{1,0},{2,3},{3,2},{4,5},{5,4},{6,7},{7,6},{8,9},{9,8},{10,11... | collective-permute-start | bytes 3145736 | tf_op jit(solution)/shard_map/ppermute | solution.py:36
  104.9 3.6 %collective-permute-start.6 = (f32[2,128,1536]{2,1,0:T(8,128)}, f32[2,128,1536]{2,1,0:T(8,128)S(1)}, u32[]{:S(2)}, u32[]{:S(2)}) collective-permute-start(f32[2,128,1536]{2,1,0:T(8,128)} %slice.46.refs_0_), channel_id=1, source_target_pairs={{0,1},{1,0},{2,3},{3,2},{4,5},{5,4},{6,7},{7,6},{8,9},{9,8},{10,11... | collective-permute-start | bytes 4718600 | tf_op jit(solution)/shard_map/ppermute | solution.py:36
  105.0 5.9 %collective-permute-start.8 = (f32[2,128,1536]{2,1,0:T(8,128)}, f32[2,128,1536]{2,1,0:T(8,128)S(1)}, u32[]{:S(2)}, u32[]{:S(2)}) collective-permute-start(f32[2,128,1536]{2,1,0:T(8,128)} %collective-permute-done.7.refs_2_), channel_id=1, source_target_pairs={{0,1},{1,0},{2,3},{3,2},{4,5},{5,4},{6,7},{7,6},{8,9},{9,8},{10,11... | collective-permute-start | bytes 4718600 | tf_op jit(solution)/shard_map/ppermute | solution.py:36
  106.5 13.9 %collective-permute-start.10 = (f32[2,128,512]{2,1,0:T(8,128)S(1)}, f32[2,128,512]{2,1,0:T(8,128)S(1)}, u32[]{:S(2)}, u32[]{:S(2)}) collective-permute-start(f32[2,128,512]{2,1,0:T(8,128)S(1)} %slice.47.refs_0_), channel_id=1, source_target_pairs={{0,2},{1,3},{2,0},{3,1},{4,6},{5,7},{6,4},{7,5},{8,10},{9,11},{10,... | collective-permute-start | bytes 1572872 | tf_op jit(solution)/shard_map/ppermute | solution.py:36
  138.0 18.7 %collective-permute-start.14 = (f32[2,2,128,256]{3,2,1,0:T(8,128)S(1)}, f32[2,2,128,256]{3,2,1,0:T(8,128)S(1)}, u32[]{:S(2)}, u32[]{:S(2)}) collective-permute-start(f32[2,2,128,256]{3,2,1,0:T(8,128)S(1)} %get-tuple-element.98), channel_id=1, source_target_pairs={{0,2},{1,3},{2,0},{3,1},{4,6},{5,7},{6,4},{7,5},{8,10},{9,11},{10,... | collective-permute-start | bytes 1572872 | tf_op jit(solution)/shard_map/ppermute | solution.py:41
  156.7 13.7 %collective-permute-start.15 = (f32[2,2,128,256]{3,2,1,0:T(8,128)S(1)}, f32[2,2,128,256]{3,2,1,0:T(8,128)S(1)}, u32[]{:S(2)}, u32[]{:S(2)}) collective-permute-start(f32[2,2,128,256]{3,2,1,0:T(8,128)S(1)} %get-tuple-element.100), channel_id=1, source_target_pairs={{0,2},{1,3},{2,0},{3,1},{4,6},{5,7},{6,4},{7,5},{8,10},{9,11},{10,... | collective-permute-start | bytes 1572872 | tf_op jit(solution)/shard_map/ppermute | solution.py:41
  170.4 26.1 %collective-permute-start.19 = (f32[2,2,256,256]{3,2,1,0:T(8,128)S(1)}, f32[2,2,256,256]{3,2,1,0:T(8,128)S(1)}, u32[]{:S(2)}, u32[]{:S(2)}) collective-permute-start(f32[2,2,256,256]{3,2,1,0:T(8,128)S(1)} %get-tuple-element.104), channel_id=1, source_target_pairs={{0,2},{1,3},{2,0},{3,1},{4,6},{5,7},{6,4},{7,5},{8,10},{9,11},{10,... | collective-permute-start | bytes 3145736 | tf_op jit(solution)/shard_map/ppermute | solution.py:41
  175.1 26.3 %collective-permute-start.30 = (f32[2,512,256]{2,1,0:T(8,128)S(1)}, f32[2,512,256]{2,1,0:T(8,128)S(1)}, u32[]{:S(2)}, u32[]{:S(2)}) collective-permute-start(f32[2,512,256]{2,1,0:T(8,128)S(1)} %get-tuple-element.126), channel_id=1, source_target_pairs={{0,4},{4,8},{8,12},{1,5},{5,9},{9,13},{2,6},{6,10},{10,14},{3,7},{... | collective-permute-start | bytes 3145736 | tf_op jit(solution)/shard_map/ppermute | solution.py:31
  178.8 38.1 %collective-permute-start.22 = (f32[2,2,256,256]{3,2,1,0:T(8,128)S(1)}, f32[2,2,256,256]{3,2,1,0:T(8,128)S(1)}, u32[]{:S(2)}, u32[]{:S(2)}) collective-permute-start(f32[2,2,256,256]{3,2,1,0:T(8,128)S(1)} %get-tuple-element.109), channel_id=1, source_target_pairs={{0,2},{1,3},{2,0},{3,1},{4,6},{5,7},{6,4},{7,5},{8,10},{9,11},{10,... | collective-permute-start | bytes 3145736 | tf_op jit(solution)/shard_map/ppermute | solution.py:41
  180.5 16.1 %collective-permute-start.18 = (f32[1,2,256,256]{3,2,1,0:T(8,128)S(1)}, f32[1,2,256,256]{3,2,1,0:T(8,128)S(1)}, u32[]{:S(2)}, u32[]{:S(2)}) collective-permute-start(f32[1,2,256,256]{3,2,1,0:T(8,128)S(1)} %slice.52), channel_id=1, source_target_pairs={{0,1},{1,0},{2,3},{3,2},{4,5},{5,4},{6,7},{7,6},{8,9},{9,8},{10,11... | collective-permute-start | bytes 1572872 | tf_op jit(solution)/shard_map/ppermute | solution.py:36
  201.5 26.3 %collective-permute-start.31 = (f32[2,512,256]{2,1,0:T(8,128)S(1)}, f32[2,512,256]{2,1,0:T(8,128)S(1)}, u32[]{:S(2)}, u32[]{:S(2)}) collective-permute-start(f32[2,512,256]{2,1,0:T(8,128)S(1)} %get-tuple-element.127), channel_id=1, source_target_pairs={{0,4},{4,8},{8,12},{1,5},{5,9},{9,13},{2,6},{6,10},{10,14},{3,7},{... | collective-permute-start | bytes 3145736 | tf_op jit(solution)/shard_map/ppermute | solution.py:31
  206.0 11.1 %collective-permute-start.21 = (f32[1,2,256,256]{3,2,1,0:T(8,128)S(1)}, f32[1,2,256,256]{3,2,1,0:T(8,128)S(1)}, u32[]{:S(2)}, u32[]{:S(2)}) collective-permute-start(f32[1,2,256,256]{3,2,1,0:T(8,128)S(1)} %slice.54), channel_id=1, source_target_pairs={{0,1},{1,0},{2,3},{3,2},{4,5},{5,4},{6,7},{7,6},{8,9},{9,8},{10,11... | collective-permute-start | bytes 1572872 | tf_op jit(solution)/shard_map/ppermute | solution.py:36
  227.7 25.3 %collective-permute-start.32 = (f32[2,512,256]{2,1,0:T(8,128)S(1)}, f32[2,512,256]{2,1,0:T(8,128)S(1)}, u32[]{:S(2)}, u32[]{:S(2)}) collective-permute-start(f32[2,512,256]{2,1,0:T(8,128)S(1)} %get-tuple-element.128), channel_id=1, source_target_pairs={{0,4},{4,8},{8,12},{1,5},{5,9},{9,13},{2,6},{6,10},{10,14},{3,7},{... | collective-permute-start | bytes 3145736 | tf_op jit(solution)/shard_map/ppermute | solution.py:31
  232.2 14.9 %collective-permute-start.25 = (f32[2,2,256,128]{3,2,1,0:T(8,128)S(1)}, f32[2,2,256,128]{3,2,1,0:T(8,128)S(1)}, u32[]{:S(2)}, u32[]{:S(2)}) collective-permute-start(f32[2,2,256,128]{3,2,1,0:T(8,128)S(1)} %get-tuple-element.114), channel_id=1, source_target_pairs={{0,2},{1,3},{2,0},{3,1},{4,6},{5,7},{6,4},{7,5},{8,10},{9,11},{10,... | collective-permute-start | bytes 1572872 | tf_op jit(solution)/shard_map/ppermute | solution.py:41
  233.8 23.8 %collective-permute-start.28 = (f32[2,2,256,128]{3,2,1,0:T(8,128)S(1)}, f32[2,2,256,128]{3,2,1,0:T(8,128)S(1)}, u32[]{:S(2)}, u32[]{:S(2)}) collective-permute-start(f32[2,2,256,128]{3,2,1,0:T(8,128)S(1)} %get-tuple-element.119), channel_id=1, source_target_pairs={{0,2},{1,3},{2,0},{3,1},{4,6},{5,7},{6,4},{7,5},{8,10},{9,11},{10,... | collective-permute-start | bytes 1572872 | tf_op jit(solution)/shard_map/ppermute | solution.py:41
  253.1 13.2 %collective-permute-start.33 = (f32[2,512,128]{2,1,0:T(8,128)S(1)}, f32[2,512,128]{2,1,0:T(8,128)S(1)}, u32[]{:S(2)}, u32[]{:S(2)}) collective-permute-start(f32[2,512,128]{2,1,0:T(8,128)S(1)} %get-tuple-element.129), channel_id=1, source_target_pairs={{0,4},{4,8},{8,12},{1,5},{5,9},{9,13},{2,6},{6,10},{10,14},{3,7},{... | collective-permute-start | bytes 1572872 | tf_op jit(solution)/shard_map/ppermute | solution.py:31
  266.2 12.3 %collective-permute-start.34 = (f32[2,512,128]{2,1,0:T(8,128)S(1)}, f32[2,512,128]{2,1,0:T(8,128)S(1)}, u32[]{:S(2)}, u32[]{:S(2)}) collective-permute-start(f32[2,512,128]{2,1,0:T(8,128)S(1)} %get-tuple-element.130), channel_id=1, source_target_pairs={{0,4},{4,8},{8,12},{1,5},{5,9},{9,13},{2,6},{6,10},{10,14},{3,7},{... | collective-permute-start | bytes 1572872 | tf_op jit(solution)/shard_map/ppermute | solution.py:31
  (36 other events, 307.0 us)
Sparse Core Ops, SparseCore 0:
  20.0 49.5 all-gather.2

commit v2 on v1

--- a/solution.py
+++ b/solution.py
@@ -12,7 +12,8 @@
 F32 = jnp.float32
 BF16 = jnp.bfloat16
 LANES = 128
-ROW_BLOCK = 16
+ROW_BLOCK = 32
+PART_ROWS = 16
 RADIX = 8
 MEBI = 1024 * 1024
 ANYWHERE = pl.BlockSpec(memory_space=pl.ANY)
@@ -177,7 +178,7 @@
     )(order, phase, *after)
 
 
-def azimuth_front_kernel(count, place_ref, high_ref, low_ref, *refs):
+def azimuth_front_kernel(count, place_ref, high_ref, low_ref, cos_ref, sin_ref, *refs):
     pieces, (out_ref, hi, lo) = refs[:count], refs[-3:]
     per = pieces[0].shape[1]
     half = hi.shape[0] // 2
@@ -188,24 +189,30 @@
             top = pl.ds(pl.multiple_of(part * half + owner * per, per), per)
             hi[top, :], lo[top, :] = split_words(pieces[q][part])
     mixed = dot(high_ref[0], hi[...]) + dot(high_ref[0], lo[...]) + dot(low_ref[0], hi[...])
-    out_ref[0] = mixed[:rows]
-    out_ref[1] = mixed[rows:]
-
-
-def azimuth_front(pieces, t, table, after=()):
+    re, im = mixed[:rows], mixed[rows:]
+    c, s = cos_ref[0], sin_ref[0]
+    out_ref[0] = re * c - im * s
+    out_ref[1] = re * s + im * c
+
+
+def azimuth_front(pieces, t, table, scaling, column):
     count = len(pieces)
     per, width = pieces[0].shape[1:]
     _, double, depth = table[0].shape
-    step = min(width, 256)
+    step = min(256, scaling[0].shape[2])
+    per_tile = scaling[0].shape[2] // step
+    first = column // step
     whole = pl.BlockSpec((1, double, depth), lambda i, t: (t[0], 0, 0))
+    turn = pl.BlockSpec(
+        (1, double // 2, step), lambda i, t: ((first + i) // per_tile, 0, (first + i) % per_tile)
+    )
     return pl.pallas_call(
         functools.partial(azimuth_front_kernel, count),
         grid_spec=pltpu.PrefetchScalarGridSpec(
             num_scalar_prefetch=1,
             grid=(width // step,),
-            in_specs=[whole, whole]
-            + [pl.BlockSpec((2, per, step), lambda i, t: (0, 0, i))] * count
-            + [ANYWHERE] * len(after),
+            in_specs=[whole, whole, turn, turn]
+            + [pl.BlockSpec((2, per, step), lambda i, t: (0, 0, i))] * count,
             out_specs=pl.BlockSpec((2, double // 2, step), lambda i, t: (0, 0, i)),
             scratch_shapes=[pltpu.VMEM((depth, step), BF16)] * 2,
         ),
@@ -213,7 +220,7 @@
         compiler_params=params(),
         cost_estimate=cost(),
         name="azimuth_front",
-    )(t, *table, *pieces, *after)
+    )(t, *table, *scaling, *pieces)
 
 
 def azimuth_front_table(tiles, pulses, rows, extent):
@@ -246,62 +253,73 @@
 def range_kernel(n_in, n_keep, tiles, widths, place_ref, *refs):
     refs = list(refs)
     u_refs = [refs.pop(0) for _ in range(n_in)]
-    cs_ref, ss_ref, cr_ref, sr_ref, front_ref, back_ref, wf_ref, wi_ref = [
-        refs.pop(0) for _ in range(8)
-    ]
+    cr_ref, sr_ref, front_ref, back_ref, wf_ref, wi_ref = [refs.pop(0) for _ in range(6)]
     del refs[:n_keep]
     outs = [[refs.pop(0) for _ in range(tiles // 2)] for _ in widths]
     core = place_ref[0] % 2
-    stage_re, stage_im, hi, lo, mid = refs
-    rows = stage_re.shape[0] * LANES // (cr_ref.shape[2])
+    parts = len(refs) // 5
+    rows = u_refs[0].shape[1] // parts
     count = cr_ref.shape[2] // LANES
-    per_tile = cs_ref.shape[2] // LANES
-
-    def load(a):
-        lane, j = place(a * LANES, [u.shape[2] for u in u_refs])
-        u = u_refs[j]
-        re, im = u[0, :, lane : lane + LANES], u[1, :, lane : lane + LANES]
-        lane = (a % per_tile) * LANES
-        c = cs_ref[a // per_tile, :, lane : lane + LANES]
-        s = ss_ref[a // per_tile, :, lane : lane + LANES]
-        return re * c - im * s, re * s + im * c
-
-    def put(k, re, im):
-        top = k * rows
-        hi[top : top + rows, :LANES], lo[top : top + rows, :LANES] = split_words(re)
-        hi[top : top + rows, LANES:], lo[top : top + rows, LANES:] = split_words(im)
-
-    def emit_front(k, value):
-        re, im = value
-        c, s = front_ref[0, k : k + 1, :], front_ref[1, k : k + 1, :]
-        put(k, re * c - im * s, re * s + im * c)
-
-    sectioned_dft(load, emit_front, count, -1, stage_re, stage_im, rows)
-    high = hi[...]
-    mid[...] = dot(jnp.concatenate([high, lo[...], high], axis=1), wf_ref[...])
-    for k in range(count):
-        top = k * rows
-        re, im = mid[top : top + rows, :LANES], mid[top : top + rows, LANES:]
-        c = cr_ref[0, :, k * LANES : (k + 1) * LANES]
-        s = sr_ref[0, :, k * LANES : (k + 1) * LANES]
-        put(k, re * c - im * s, re * s + im * c)
-    high = hi[...]
-    mid[...] = dot(jnp.concatenate([high, lo[...], high], axis=1), wi_ref[...])
-
-    def load_back(k):
-        top = k * rows
-        re, im = mid[top : top + rows, :LANES], mid[top : top + rows, LANES:]
-        c, s = back_ref[0, k : k + 1, :], back_ref[1, k : k + 1, :]
-        return re * c - im * s, re * s + im * c
-
-    def emit_back(a, value):
-        lane, j = place((a % per_tile) * LANES, widths)
-        tile = a // per_tile
-        out, toward = outs[j][tile // 2], (tile % 2) ^ core
-        out[toward, 0, :, lane : lane + LANES] = value[0]
-        out[toward, 1, :, lane : lane + LANES] = value[1]
-
-    sectioned_dft(load_back, emit_back, count, 1, stage_re, stage_im, rows)
+    per_tile = count // tiles
+    sizes = [u.shape[2] for u in u_refs]
+
+    def steps_of(part):
+        stage_re, stage_im, hi, lo, mid = refs[5 * part : 5 * part + 5]
+        here = slice(part * rows, (part + 1) * rows)
+
+        def load(a):
+            lane, j = place(a * LANES, sizes)
+            u = u_refs[j]
+            return u[0, here, lane : lane + LANES], u[1, here, lane : lane + LANES]
+
+        def put(k, re, im):
+            top = k * rows
+            hi[top : top + rows, :LANES], lo[top : top + rows, :LANES] = split_words(re)
+            hi[top : top + rows, LANES:], lo[top : top + rows, LANES:] = split_words(im)
+
+        def emit_front(k, value):
+            re, im = value
+            c, s = front_ref[0, k : k + 1, :], front_ref[1, k : k + 1, :]
+            put(k, re * c - im * s, re * s + im * c)
+
+        def front():
+            sectioned_dft(load, emit_front, count, -1, stage_re, stage_im, rows)
+
+        def mix(table_ref):
+            high = hi[...]
+            mid[...] = dot(jnp.concatenate([high, lo[...], high], axis=1), table_ref[...])
+
+        def filtered():
+            for k in range(count):
+                top = k * rows
+                re, im = mid[top : top + rows, :LANES], mid[top : top + rows, LANES:]
+                c = cr_ref[0, here, k * LANES : (k + 1) * LANES]
+                s = sr_ref[0, here, k * LANES : (k + 1) * LANES]
+                put(k, re * c - im * s, re * s + im * c)
+
+        def load_back(k):
+            top = k * rows
+            re, im = mid[top : top + rows, :LANES], mid[top : top + rows, LANES:]
+            c, s = back_ref[0, k : k + 1, :], back_ref[1, k : k + 1, :]
+            return re * c - im * s, re * s + im * c
+
+        def emit_back(a, value):
+            lane, j = place((a % per_tile) * LANES, widths)
+            tile = a // per_tile
+            out, toward = outs[j][tile // 2], (tile % 2) ^ core
+            out[toward, 0, here, lane : lane + LANES] = value[0]
+            out[toward, 1, here, lane : lane + LANES] = value[1]
+
+        def back():
+            sectioned_dft(load_back, emit_back, count, 1, stage_re, stage_im, rows)
+
+        return [front, lambda: mix(wf_ref), filtered, lambda: mix(wi_ref), back]
+
+    work = [steps_of(part) for part in range(parts)]
+    for at in range(5 + 2 * parts):
+        for part in range(parts):
+            if 0 <= at - part < 5:
+                work[part][at - part]()
 
 
 def range_tables(t, tiles, count):
@@ -323,9 +341,8 @@
     return jnp.asarray(np.concatenate([high, high, low], axis=0))
 
 
-def range_pass(spectra, t, scaling, ranging, front, back, span, split, widths, earlier, after):
+def range_pass(spectra, t, tiles, ranging, front, back, span, split, widths, earlier, after):
     rows = spectra[0].shape[1]
-    tiles, _, width = scaling[0].shape
     extent = ranging[0].shape[2]
     count = extent // LANES
     block = ROW_BLOCK
@@ -334,7 +351,6 @@
     in_specs = [
         pl.BlockSpec((2, block, u.shape[2]), lambda i, t: (0, first + i, 0)) for u in spectra
     ]
-    in_specs += [pl.BlockSpec((tiles, block, width), lambda i, t: (0, first + i, 0))] * 2
     in_specs += [pl.BlockSpec((1, block, extent), lambda i, t: (0, first + i, 0))] * 2
     in_specs += [pl.BlockSpec((2, count, LANES), lambda i, t: (0, 0, 0))] * 2
     in_specs += [pl.BlockSpec(wf.shape, lambda i, t: (0, 0))] * 2
@@ -359,19 +375,20 @@
             in_specs=in_specs,
             out_specs=out_specs,
             scratch_shapes=[
-                pltpu.VMEM((count * block, LANES), F32),
-                pltpu.VMEM((count * block, LANES), F32),
-                pltpu.VMEM((count * block, 2 * LANES), BF16),
-                pltpu.VMEM((count * block, 2 * LANES), BF16),
-                pltpu.VMEM((count * block, 2 * LANES), F32),
-            ],
+                pltpu.VMEM((count * PART_ROWS, LANES), F32),
+                pltpu.VMEM((count * PART_ROWS, LANES), F32),
+                pltpu.VMEM((count * PART_ROWS, 2 * LANES), BF16),
+                pltpu.VMEM((count * PART_ROWS, 2 * LANES), BF16),
+                pltpu.VMEM((count * PART_ROWS, 2 * LANES), F32),
+            ]
+            * (block // PART_ROWS),
         ),
         out_shape=out_shape,
         input_output_aliases=aliases,
         compiler_params=params(),
         cost_estimate=cost(),
         name="range_filter",
-    )(t, *spectra, *scaling, *ranging, front, back, wf, wi, *earlier, *after)
+    )(t, *spectra, *ranging, front, back, wf, wi, *earlier, *after)
     return [flat[j * chips : (j + 1) * chips] for j in range(len(widths))]
 
 
@@ -409,8 +426,8 @@
             for a in range(RADIX)
         ]
         for p, value in enumerate(short_dft(values, 1)):
+            top = (p % half) * mixed_rows + low
             ref = head_ref if p < half else tail_ref
-            top = (p % half) * mixed_rows + low
             ref[0, top : top + 8, :] = value[0]
             ref[1, top : top + 8, :] = value[1]
 
@@ -421,8 +438,7 @@
     width = flat[0].shape[3]
     tiles, rows, _ = turns[0].shape
     double = table[0].shape[1]
-    out_rows = RADIX * double // 4
-    out = jax.ShapeDtypeStruct((2, out_rows, width), F32)
+    outs = [jax.ShapeDtypeStruct((2, RADIX * double // 4, width), F32)] * 2
     whole = pl.BlockSpec(table[0].shape, lambda i, t: (0, 0, 0))
     turn = pl.BlockSpec((tiles, rows, width), lambda i, t: (0, 0, column // width))
     return pl.pallas_call(
@@ -433,13 +449,13 @@
             in_specs=[whole, whole, turn, turn]
             + [pl.BlockSpec((1, *piece.shape[1:]), lambda i, t: (0, 0, 0, 0)) for piece in flat]
             + [ANYWHERE] * len(after),
-            out_specs=[pl.BlockSpec((2, out_rows, width), lambda i, t: (0, 0, 0))] * 2,
+            out_specs=[pl.BlockSpec(out.shape, lambda i, t: (0, 0, 0)) for out in outs],
             scratch_shapes=[
                 pltpu.VMEM((2, double // 2, width), F32),
                 pltpu.VMEM((RADIX, double, width), F32),
             ],
         ),
-        out_shape=[out, out],
+        out_shape=outs,
         compiler_params=params(24),
         cost_estimate=cost(),
         name="azimuth_back",
@@ -460,13 +476,13 @@
 
 def add_tail(head, tail, earlier, column, full_width):
     _, rows, width = head.shape
-    spec = pl.BlockSpec((1, rows, width), lambda i: (i, 0, 0))
     kept = [] if earlier is None else [earlier]
     return pl.pallas_call(
         add_kernel,
-        grid=(2,),
-        in_specs=[spec, spec] + [ANYWHERE] * len(kept),
-        out_specs=pl.BlockSpec((1, rows, width), lambda i: (i, 0, column // width)),
+        grid=(1,),
+        in_specs=[pl.BlockSpec((2, rows, width), lambda i: (0, 0, 0))] * 2
+        + [ANYWHERE] * len(kept),
+        out_specs=pl.BlockSpec((2, rows, width), lambda i: (0, 0, column // width)),
         out_shape=jax.ShapeDtypeStruct((2, rows, full_width), F32),
         input_output_aliases={2: 0} if kept else {},
         compiler_params=params(),
@@ -488,6 +504,12 @@
     near = [rows_at((t ^ q) * rows, rows) for q in range(2)]
     far = [rows_at((t ^ q) * rows + replica * share, share) for q in range(2, tiles)]
     return near, far
+
+
+def halves(piece):
+    rows = piece.shape[2]
+    cut = rows // 2 if rows >= 256 else rows
+    return [piece[1:, :, low : low + cut] for low in range(0, rows, cut)]
 
 
 def body(raw_echo, phase_scaling, phase_range, phase_azimuth):
@@ -503,9 +525,9 @@
     near, far = scaling_cuts(phase_scaling, rows)
     far_sent = [exchange(cut, q + 2) for q, cut in enumerate(far)]
 
-    eighth = ranges // 8
+    part = ranges // 8
     straight, at = [], 0
-    for size in (4 * eighth, 3 * eighth, eighth):
+    for size in (4 * part, 3 * part, part):
         piece = gate(raw_echo[:, :, at : at + size], *far_sent)
         at += size
         straight.append([piece] + [exchange(piece, q) for q in range(2, tiles, 2)])
@@ -521,59 +543,58 @@
     back_table = azimuth_back_table(extent)
 
     tokens = [azimuth[0], front, back]
-    spectra = []
-    for j, received in enumerate(straight):
+    far_rows = gate(far_all, *tokens).transpose(1, 0, 2, 3).reshape(tiles - 2, rows, width)
+    pieces = jnp.concatenate([near[0][None], near[1][None], far_rows])
+    scaling = turns_of(pieces, t ^ index, after=[azimuth[0]])
+    spectra, column = [], 0
+    for received in straight:
         received = [gate(piece, *tokens) for piece in received]
         handed = [exchange(piece, 1) for piece in received]
         got = [piece for pair in zip(received, handed) for piece in pair]
-        spectra.append(azimuth_front(got, place_t, front_table))
+        spectra.append(azimuth_front(got, place_t, front_table, scaling, column))
+        column += received[0].shape[2]
         tokens = [spectra[-1]]
-        if j == 0:
-            far_rows = gate(far_all, *tokens).transpose(1, 0, 2, 3)
-            far_rows = far_rows.reshape(tiles - 2, rows, width)
-            pieces = jnp.concatenate([near[0][None], near[1][None], far_rows])
-            scaling = turns_of(pieces, t ^ index)
-            tokens = [scaling[0]]
 
     if width >= 8 * LANES:
-        widths = [width // 4] * 3 + [width // 8] * 2
+        widths = [width // 4] * 4
     else:
         widths = [LANES] * (width // LANES)
     blocks = rows // ROW_BLOCK
-    spans = [(0, blocks)] if blocks < 16 else [(0, blocks // 2), (blocks // 2, blocks // 2)]
+    spans = [(0, blocks)] if blocks < 8 else [(0, blocks // 2), (blocks // 2, blocks // 2)]
     split = 1 if len(spans) > 1 else 0
     parts, kept, sequence = [], [], []
     for span in spans:
         done = range_pass(
-            spectra, place_t, scaling, ranging, front, back, span, split, widths, kept, []
+            spectra, place_t, tiles, ranging, front, back, span, split, widths, kept, []
         )
         parts.append([to_chips(chunk, sequence, 1) for chunk in done[:split]])
         kept = [piece for chunk in done[split:] for piece in chunk]
-    arrived = [[part[j] for part in parts] for j in range(split)]
+    ready = [[part[j] for part in parts] for j in range(split)]
     for j, chunk in enumerate(done[split:]):
-        arrived.append([to_chips(chunk, sequence, 1 if j == 0 else 2)])
+        ready.append([to_chips(chunk, sequence, min(j + 1, 2))])
 
     heads, tails, images, column = [], [], [], 0
-    for j, groups in enumerate(arrived):
-        groups = [[gate(piece, *heads[-1:]) for piece in group] for group in groups]
+    for j in range(len(widths)):
+        tokens = heads[-1:] + tails[j - 2 : j - 1] if j >= 2 else heads[-1:]
+        groups = [[gate(piece, *tokens) for piece in group] for group in ready[j]]
         pieces = []
         for k in range(tiles // 2):
             pieces.append([group[k] for group in groups])
-            pieces.append([exchange(group[k][1:], 1) for group in groups])
-        before = heads[-1:]
-        head, tail = azimuth_back(pieces, place_t, azimuth, back_table, column, after=before)
+            pieces.append([exchange(part, 1) for group in groups for part in halves(group[k])])
+        head, tail = azimuth_back(
+            pieces, place_t, azimuth, back_table, column, after=heads[-1:]
+        )
         heads.append(head)
-        tokens = [tails[-1][0]] if tails else []
-        tails.append((from_behind(gate(tail, *tokens), "az"), column))
+        tokens = tails[-1:] if j == len(widths) - 1 else []
+        tails.append(from_behind(gate(tail, *tokens), "az"))
+        if j >= 1:
+            image = images[-1] if images else None
+            images.append(
+                add_tail(heads[j - 1], tails[j - 1], image, column - widths[j - 1], width)
+            )
         column += widths[j]
-        if j >= 2:
-            tail, at = tails[j - 2]
-            image = images[-1] if images else None
-            images.append(add_tail(heads[j - 2], tail, image, at, width))
-    for j in range(len(images), len(heads)):
-        tail, at = tails[j]
-        images.append(add_tail(heads[j], tail, images[-1] if images else None, at, width))
-    return images[-1]
+    image = images[-1] if images else None
+    return add_tail(heads[-1], tails[-1], image, column - widths[-1], width)
 
 
 def solution(mesh):

time: 287 us -> 276 us (0.962)
  waiting for transfers between devices: 104 us -> 112 us
  Pallas kernels: 78.1 us -> 70.4 us
  local copies, waits for them, and re-layouts: 46.9 us -> 40.2 us
  starting transfers between devices: 40.5 us -> 36.5 us
    ppermute x5 -> x4, waiting for transfers between devices: 20.7 us -> 34.1 us  [from_behind(): return lax.ppermute(value, axis, [(i, i + 1) for i in range(length - 1)])]
    pallas_call x2, Pallas kernels: 24.8 us -> 17 us  [range_pass(): pl.pallas_call(functools.partial(range_kernel, len(spectra), len(earlier)...]
    unnamed x49 -> x39, local copies, waits for them, and re-layouts: 24.5 us -> 17.8 us
    ppermute x6 -> x5, waiting for transfers between devices: 53.1 us -> 47.4 us  [shift(): lax.ppermute(value, 'tile', [(i, (i + by) % length) for i in range(length)])]
    ppermute x5 -> x4, starting transfers between devices: 21.4 us -> 16.1 us  [from_behind(): return lax.ppermute(value, axis, [(i, i + 1) for i in range(length - 1)])]
    ppermute x24 -> x28, starting transfers between devices: 13 us -> 14.1 us  [exchange(): return lax.ppermute(value, 'tile', [(i, i ^ mask) for i in range(length)])]
    pallas_call x5 -> x4, Pallas kernels: 7.22 us -> 6.66 us  [azimuth_back(): pl.pallas_call(functools.partial(azimuth_back_kernel, layout), grid_spec=...]
    ppermute x6 -> x5, starting transfers between devices: 6.19 us -> 6.3 us  [shift(): lax.ppermute(value, 'tile', [(i, (i + by) % length) for i in range(length)])]
  transfers between devices with their start and end apart: 36 -> 38, of which waited for: 28 -> 27; matrix products, arithmetic and copies ran while one was open for 10% -> 11% of each run, Pallas kernels for 22% -> 21%
where the time goes in v2:
time: 276 us; the launch traced here: 275 us
  waiting for transfers between devices  112 us (41%)
  Pallas kernels  70.4 us (26%)
  local copies, waits for them, and re-layouts  40.2 us (15%)
  starting transfers between devices  36.5 us (13%)
  between operations  13.9 us (5%)
  other arithmetic  2.78 us (1%)
    ppermute x5, waiting for transfers between devices, shift(): lax.ppermute(value, 'tile', [(i, (i + by) % length) for i in range(length)])  47.4 us
    ppermute x4, waiting for transfers between devices, from_behind(): return lax.ppermute(value, axis, [(i, i + 1) for i in range(length - 1)])  34.1 us
    ppermute x28, waiting for transfers between devices, exchange(): return lax.ppermute(value, 'tile', [(i, i ^ mask) for i in range(length)])  30.2 us
    pallas_call x3, Pallas kernels, azimuth_front(): pl.pallas_call(functools.partial(azimuth_front_kernel, count), grid_spec=...  22.5 us
    pallas_call x3, Pallas kernels, turns_of(): pl.pallas_call(turn_kernel, grid_spec=pltpu.PrefetchScalarGridSpec(num_sc...  19.9 us
    unnamed x39, local copies, waits for them, and re-layouts  17.8 us
    pallas_call x2, Pallas kernels, range_pass(): pl.pallas_call(functools.partial(range_kernel, len(spectra), len(earlier)...  17 us
    ppermute x4, starting transfers between devices, from_behind(): return lax.ppermute(value, axis, [(i, i + 1) for i in range(length - 1)])  16.1 us
  transfers between devices with their start and end apart: 38, of which 27 were waited for; matrix products, arithmetic and copies ran while one was open for 11% of the time, Pallas kernels for 21%

profile of v2, /device:TPU:0, one launch (start us, length us, event | category | flops | bytes accessed | tf_op | source)
XLA Modules:
  0.0 275.4 jit_solution(17521508628708960685)
XLA Ops:
  19.9 5.6 %copy.27 = f32[256,4096]{0,1:T(8,128)} copy(f32[256,4096]{1,0:T(8,128)} %param.14) | data formatting | bytes 8388608 | tf_op args[2]
  25.5 6.0 %copy.28 = f32[256,32,128]{2,1,0:T(8,128)} copy(f32[256,32,128]{0,1,2:T(8,128)} %bitcast.15) | data formatting | bytes 8388608 | tf_op jit(solution)/shard_map/transpose | solution.py:538
  31.6 4.9 %reshape.190.phase_ref = f32[1,256,4096]{2,1,0:T(8,128)} reshape(f32[256,32,128]{2,1,0:T(8,128)} %copy.28) | data formatting | bytes 8388608 | tf_op jit(solution)/shard_map/reshape | solution.py:538
  38.7 6.2 %phase_turns.3 = (f32[1,256,4096]{2,1,0:T(8,128)S(1)}, f32[1,256,4096]{2,1,0:T(8,128)S(1)}) custom-call(s32[1]{0:T(128)} %constant.62.clone.1.order_ref, f32[1,256,4096]{2,1,0:T(8,128)S(1)} %copy-done.11), custom_call_target="tpu_custom_call" | custom-call | flops 1024 | bytes 1024 | tf_op jit(solution)/shard_map/phase_turns/pallas_call | solution.py:164
  47.0 6.8 %phase_turns.4 = (f32[4,256,1024]{2,1,0:T(8,128)S(1)}, f32[4,256,1024]{2,1,0:T(8,128)S(1)}) custom-call(s32[4]{0:T(128)S(1)} %iota.34.order_ref, f32[4,256,1024]{2,1,0:T(8,128)S(1)} %bitcast.14, f32[1,256,4096]{2,1,0:T(8,128)S(1)} %get-tuple-element.56.refs_0_.refs_3_), custom_call_target="tpu_custom_call" | custom-call | flops 1024 | bytes 1024 | tf_op jit(solution)/shard_map/phase_turns/pallas_call | solution.py:164
  60.2 4.9 %collective-permute-done.4.refs_2_ = f32[2,128,2048]{2,1,0:T(8,128)} collective-permute-done((f32[2,128,2048]{2,1,0:T(8,128)S(1)}, f32[2,128,2048]{2,1,0:T(8,128)}, u32[]{:S(2)}, u32[]{:S(2)}) %collective-permute-start.4) | collective-permute-done | bytes 2097184 | tf_op jit(solution)/shard_map/ppermute | solution.py:37
  77.9 6.8 %phase_turns.5 = (f32[4,256,1024]{2,1,0:T(8,128)S(1)}, f32[4,256,1024]{2,1,0:T(8,128)S(1)}) custom-call(s32[4]{0:T(128)S(1)} %iota_xor_fusion.order_ref, f32[4,256,1024]{2,1,0:T(8,128)S(1)} %pad_maximum_fusion.phase_ref, f32[4,256,1024]{2,1,0:T(8,128)S(1)} %copy-done.1), custom_call_target="tpu_custom_call" | custom-call | flops 1024 | bytes 1024 | tf_op jit(solution)/shard_map/phase_turns/pallas_call | solution.py:164
  84.8 11.3 %azimuth_front.3.refs_0_ = f32[2,256,2048]{2,1,0:T(8,128)S(1)} custom-call(s32[1]{0:T(128)} %bitcast.place_ref, bf16[4,512,1024]{2,1,0:T(8,128)(2,1)S(1)} %copy-done.6, bf16[4,512,1024]{2,1,0:T(8,128)(2,1)S(1)} %copy-done.7, f32[4,256,1024]{2,1,0:T(8,128)S(1)} %get-tuple-element.60.cos_ref, f32[4,256,1024]{2,1,0:T(8,128)S(1)} %get-tuple-element.61.sin_ref, ...), custom_call_target="tpu_custom_call" | custom-call | flops 1024 | bytes 1024 | tf_op jit(solution)/shard_map/azimuth_front/pallas_call | solution.py:209
  96.4 8.6 %collective-permute-done.7.refs_2_ = f32[2,128,1536]{2,1,0:T(8,128)} collective-permute-done((f32[2,128,1536]{2,1,0:T(8,128)}, f32[2,128,1536]{2,1,0:T(8,128)}, u32[]{:S(2)}, u32[]{:S(2)}) %collective-permute-start.7) | collective-permute-done | bytes 1572896 | tf_op jit(solution)/shard_map/ppermute | solution.py:37
  108.6 8.6 %azimuth_front.4.refs_1_ = f32[2,256,1536]{2,1,0:T(8,128)S(1)} custom-call(s32[1]{0:T(128)} %bitcast.place_ref, bf16[4,512,1024]{2,1,0:T(8,128)(2,1)S(1)} %copy-done.6, bf16[4,512,1024]{2,1,0:T(8,128)(2,1)S(1)} %copy-done.7, f32[4,256,1024]{2,1,0:T(8,128)S(1)} %get-tuple-element.60.cos_ref, f32[4,256,1024]{2,1,0:T(8,128)S(1)} %get-tuple-element.61.sin_ref, ...), custom_call_target="tpu_custom_call" | custom-call | flops 1024 | bytes 1024 | tf_op jit(solution)/shard_map/azimuth_front/pallas_call | solution.py:209
  117.5 3.0 %collective-permute-done.10.refs_2_ = f32[2,128,512]{2,1,0:T(8,128)S(1)} collective-permute-done((f32[2,128,512]{2,1,0:T(8,128)S(1)}, f32[2,128,512]{2,1,0:T(8,128)S(1)}, u32[]{:S(2)}, u32[]{:S(2)}) %collective-permute-start.10) | collective-permute-done | bytes 524320 | tf_op jit(solution)/shard_map/ppermute | solution.py:37
  125.1 8.5 %range_filter.2 = (f32[2,2,128,256]{3,2,1,0:T(8,128)S(1)}, f32[2,2,128,256]{3,2,1,0:T(8,128)S(1)}, f32[2,2,256,256]{3,2,1,0:T(8,128)S(1)}, f32[2,2,256,256]{3,2,...) custom-call(s32[1]{0:T(128)} %bitcast.place_ref, ...), custom_call_target="tpu_custom_call" | custom-call | flops 1024 | bytes 1024 | tf_op jit(solution)/shard_map/range_filter/pallas_call | solution.py:370
  136.7 8.5 %range_filter.3 = (f32[2,2,128,256]{3,2,1,0:T(8,128)S(1)}, f32[2,2,128,256]{3,2,1,0:T(8,128)S(1)}, f32[2,2,256,256]{3,2,1,0:T(8,128)S(1)}, f32[2,2,256,256]{3,2,...) custom-call(s32[1]{0:T(128)} %bitcast.place_ref, ...), custom_call_target="tpu_custom_call", output_to_operand_aliasing={{2}: (10, {}), {3}: (11, {}), {4}: (12, {}), {5}: (13, {}),... | custom-call | flops 1024 | bytes 1024 | tf_op jit(solution)/shard_map/range_filter/pallas_call | solution.py:370
  149.4 11.4 %collective-permute-done.15.refs_5_ = f32[2,2,128,256]{3,2,1,0:T(8,128)S(1)} collective-permute-done((f32[2,2,128,256]{3,2,1,0:T(8,128)S(1)}, f32[2,2,128,256]{3,2,1,0:T(8,128)S(1)}, u32[]{:S(2)}, u32[]{:S(2)}) %collective-permute-start.15) | collective-permute-done | bytes 524320 | tf_op jit(solution)/shard_map/ppermute | solution.py:42
  167.0 3.6 %collective-permute-start.23 = (f32[2,512,256]{2,1,0:T(8,128)S(1)}, f32[2,512,256]{2,1,0:T(8,128)S(1)}, u32[]{:S(2)}, u32[]{:S(2)}) collective-permute-start(f32[2,512,256]{2,1,0:T(8,128)S(1)} %get-tuple-element.92), channel_id=1, source_target_pairs={{0,4},{4,8},{8,12},{1,5},{5,9},{9,13},{2,6},{6,10},{10,14},{3,7},{... | collective-permute-start | bytes 3145736 | tf_op jit(solution)/shard_map/ppermute | solution.py:32
  171.7 15.2 %collective-permute-done.20.refs_3_ = f32[2,2,256,256]{3,2,1,0:T(8,128)S(1)} collective-permute-done((f32[2,2,256,256]{3,2,1,0:T(8,128)S(1)}, f32[2,2,256,256]{3,2,1,0:T(8,128)S(1)}, u32[]{:S(2)}, u32[]{:S(2)}) %collective-permute-start.20) | collective-permute-done | bytes 1048608 | tf_op jit(solution)/shard_map/ppermute | solution.py:42
  193.3 4.4 %collective-permute-start.29 = (f32[2,512,256]{2,1,0:T(8,128)S(1)}, f32[2,512,256]{2,1,0:T(8,128)S(1)}, u32[]{:S(2)}, u32[]{:S(2)}) collective-permute-start(f32[2,512,256]{2,1,0:T(8,128)S(1)} %get-tuple-element.98), channel_id=1, source_target_pairs={{0,4},{4,8},{8,12},{1,5},{5,9},{9,13},{2,6},{6,10},{10,14},{3,7},{... | collective-permute-start | bytes 3145736 | tf_op jit(solution)/shard_map/ppermute | solution.py:32
  198.5 10.9 %collective-permute-done.26.refs_3_ = f32[2,2,256,256]{3,2,1,0:T(8,128)S(1)} collective-permute-done((f32[2,2,256,256]{3,2,1,0:T(8,128)S(1)}, f32[2,2,256,256]{3,2,1,0:T(8,128)S(1)}, u32[]{:S(2)}, u32[]{:S(2)}) %collective-permute-start.26) | collective-permute-done | bytes 1048608 | tf_op jit(solution)/shard_map/ppermute | solution.py:42
  213.1 3.7 %collective-permute-start.35 = (f32[2,512,256]{2,1,0:T(8,128)S(1)}, f32[2,512,256]{2,1,0:T(8,128)S(1)}, u32[]{:S(2)}, u32[]{:S(2)}) collective-permute-start(f32[2,512,256]{2,1,0:T(8,128)S(1)} %get-tuple-element.105), channel_id=1, source_target_pairs={{0,4},{4,8},{8,12},{1,5},{5,9},{9,13},{2,6},{6,10},{10,14},{3,7},{... | collective-permute-start | bytes 3145736 | tf_op jit(solution)/shard_map/ppermute | solution.py:32
  216.8 4.5 %collective-permute-done.29.tail_ref = f32[2,512,256]{2,1,0:T(8,128)S(1)} collective-permute-done((f32[2,512,256]{2,1,0:T(8,128)S(1)}, f32[2,512,256]{2,1,0:T(8,128)S(1)}, u32[]{:S(2)}, u32[]{:S(2)}) %collective-permute-start.29) | collective-permute-done | bytes 1048608 | tf_op jit(solution)/shard_map/ppermute | solution.py:32
  221.9 7.3 %collective-permute-done.32.refs_3_ = f32[2,2,256,256]{3,2,1,0:T(8,128)S(1)} collective-permute-done((f32[2,2,256,256]{3,2,1,0:T(8,128)S(1)}, f32[2,2,256,256]{3,2,1,0:T(8,128)S(1)}, u32[]{:S(2)}, u32[]{:S(2)}) %collective-permute-start.32) | collective-permute-done | bytes 1048608 | tf_op jit(solution)/shard_map/ppermute | solution.py:42
  232.9 9.2 %collective-permute-done.35.tail_ref = f32[2,512,256]{2,1,0:T(8,128)S(1)} collective-permute-done((f32[2,512,256]{2,1,0:T(8,128)S(1)}, f32[2,512,256]{2,1,0:T(8,128)S(1)}, u32[]{:S(2)}, u32[]{:S(2)}) %collective-permute-start.35) | collective-permute-done | bytes 1048608 | tf_op jit(solution)/shard_map/ppermute | solution.py:32
  242.1 4.4 %collective-permute-start.36 = (f32[2,512,256]{2,1,0:T(8,128)S(1)}, f32[2,512,256]{2,1,0:T(8,128)S(1)}, u32[]{:S(2)}, u32[]{:S(2)}) collective-permute-start(f32[2,512,256]{2,1,0:T(8,128)S(1)} %get-tuple-element.106), channel_id=1, source_target_pairs={{0,4},{4,8},{8,12},{1,5},{5,9},{9,13},{2,6},{6,10},{10,14},{3,7},{... | collective-permute-start | bytes 3145736 | tf_op jit(solution)/shard_map/ppermute | solution.py:32
  249.8 17.7 %collective-permute-done.36.tail_ref = f32[2,512,256]{2,1,0:T(8,128)S(1)} collective-permute-done((f32[2,512,256]{2,1,0:T(8,128)S(1)}, f32[2,512,256]{2,1,0:T(8,128)S(1)}, u32[]{:S(2)}, u32[]{:S(2)}) %collective-permute-start.36) | collective-permute-done | bytes 1048608 | tf_op jit(solution)/shard_map/ppermute | solution.py:32
  (135 shorter events, 79.3 us)
Async XLA Ops:
  6.5 66.1 %all-gather.3.cloned.1.call-start = ((), (), s32[]{:S(2)}) async-start(), calls=%async_computation | async-start | bytes 2359296 | tf_op jit(solution)/shard_map/all_gather | solution.py:535
  7.5 6.4 %collective-permute-start.2 = (f32[32,1024]{1,0:T(8,128)S(1)}, f32[32,1024]{1,0:T(8,128)S(1)}, u32[]{:S(2)}, u32[]{:S(2)}) collective-permute-start(f32[32,1024]{1,0:T(8,128)S(1)} %get-tuple-element.110), channel_id=1, source_target_pairs={{0,3},{1,2},{2,1},{3,0},{4,7},{5,6},{6,5},{7,4},{8,11},{9,10},{10,... | collective-permute-start | bytes 393224 | tf_op jit(solution)/shard_map/ppermute | solution.py:37
  10.0 6.9 %collective-permute-start.1 = (f32[32,1024]{1,0:T(8,128)S(1)}, f32[32,1024]{1,0:T(8,128)S(1)}, u32[]{:S(2)}, u32[]{:S(2)}) collective-permute-start(f32[32,1024]{1,0:T(8,128)S(1)} %get-tuple-element.109), channel_id=1, source_target_pairs={{0,2},{1,3},{2,0},{3,1},{4,6},{5,7},{6,4},{7,5},{8,10},{9,11},{10,... | collective-permute-start | bytes 393224 | tf_op jit(solution)/shard_map/ppermute | solution.py:37
  16.9 48.3 %collective-permute-start.4 = (f32[2,128,2048]{2,1,0:T(8,128)S(1)}, f32[2,128,2048]{2,1,0:T(8,128)}, u32[]{:S(2)}, u32[]{:S(2)}) collective-permute-start(f32[2,128,2048]{2,1,0:T(8,128)S(1)} %slice.57.refs_0_), channel_id=1, source_target_pairs={{0,2},{1,3},{2,0},{3,1},{4,6},{5,7},{6,4},{7,5},{8,10},{9,11},{10,... | collective-permute-start | bytes 6291464 | tf_op jit(solution)/shard_map/ppermute | solution.py:37
  60.1 24.6 %collective-permute-start.3 = (f32[2,128,2048]{2,1,0:T(8,128)S(1)}, f32[2,128,2048]{2,1,0:T(8,128)}, u32[]{:S(2)}, u32[]{:S(2)}) collective-permute-start(f32[2,128,2048]{2,1,0:T(8,128)S(1)} %slice.57.refs_0_), channel_id=1, source_target_pairs={{0,1},{1,0},{2,3},{3,2},{4,5},{5,4},{6,7},{7,6},{8,9},{9,8},{10,11... | collective-permute-start | bytes 6291464 | tf_op jit(solution)/shard_map/ppermute | solution.py:37
  65.2 19.6 %collective-permute-start.5 = (f32[2,128,2048]{2,1,0:T(8,128)}, f32[2,128,2048]{2,1,0:T(8,128)}, u32[]{:S(2)}, u32[]{:S(2)}) collective-permute-start(f32[2,128,2048]{2,1,0:T(8,128)} %collective-permute-done.4.refs_2_), channel_id=1, source_target_pairs={{0,1},{1,0},{2,3},{3,2},{4,5},{5,4},{6,7},{7,6},{8,9},{9,8},{10,11... | collective-permute-start | bytes 6291464 | tf_op jit(solution)/shard_map/ppermute | solution.py:37
  67.9 37.1 %collective-permute-start.7 = (f32[2,128,1536]{2,1,0:T(8,128)}, f32[2,128,1536]{2,1,0:T(8,128)}, u32[]{:S(2)}, u32[]{:S(2)}) collective-permute-start(f32[2,128,1536]{2,1,0:T(8,128)} %slice.58.refs_0_), channel_id=1, source_target_pairs={{0,2},{1,3},{2,0},{3,1},{4,6},{5,7},{6,4},{7,5},{8,10},{9,11},{10,... | collective-permute-start | bytes 4718600 | tf_op jit(solution)/shard_map/ppermute | solution.py:37
  96.1 11.8 %collective-permute-start.6 = (f32[2,128,1536]{2,1,0:T(8,128)}, f32[2,128,1536]{2,1,0:T(8,128)S(1)}, u32[]{:S(2)}, u32[]{:S(2)}) collective-permute-start(f32[2,128,1536]{2,1,0:T(8,128)} %slice.58.refs_0_), channel_id=1, source_target_pairs={{0,1},{1,0},{2,3},{3,2},{4,5},{5,4},{6,7},{7,6},{8,9},{9,8},{10,11... | collective-permute-start | bytes 4718600 | tf_op jit(solution)/shard_map/ppermute | solution.py:37
  106.1 14.4 %collective-permute-start.10 = (f32[2,128,512]{2,1,0:T(8,128)S(1)}, f32[2,128,512]{2,1,0:T(8,128)S(1)}, u32[]{:S(2)}, u32[]{:S(2)}) collective-permute-start(f32[2,128,512]{2,1,0:T(8,128)S(1)} %slice.59.refs_0_), channel_id=1, source_target_pairs={{0,2},{1,3},{2,0},{3,1},{4,6},{5,7},{6,4},{7,5},{8,10},{9,11},{10,... | collective-permute-start | bytes 1572872 | tf_op jit(solution)/shard_map/ppermute | solution.py:37
  133.6 14.0 %collective-permute-start.14 = (f32[2,2,128,256]{3,2,1,0:T(8,128)S(1)}, f32[2,2,128,256]{3,2,1,0:T(8,128)S(1)}, u32[]{:S(2)}, u32[]{:S(2)}) collective-permute-start(f32[2,2,128,256]{3,2,1,0:T(8,128)S(1)} %get-tuple-element.83), channel_id=1, source_target_pairs={{0,2},{1,3},{2,0},{3,1},{4,6},{5,7},{6,4},{7,5},{8,10},{9,11},{10,... | collective-permute-start | bytes 1572872 | tf_op jit(solution)/shard_map/ppermute | solution.py:42
  147.7 13.1 %collective-permute-start.15 = (f32[2,2,128,256]{3,2,1,0:T(8,128)S(1)}, f32[2,2,128,256]{3,2,1,0:T(8,128)S(1)}, u32[]{:S(2)}, u32[]{:S(2)}) collective-permute-start(f32[2,2,128,256]{3,2,1,0:T(8,128)S(1)} %get-tuple-element.85), channel_id=1, source_target_pairs={{0,2},{1,3},{2,0},{3,1},{4,6},{5,7},{6,4},{7,5},{8,10},{9,11},{10,... | collective-permute-start | bytes 1572872 | tf_op jit(solution)/shard_map/ppermute | solution.py:42
  160.8 26.1 %collective-permute-start.20 = (f32[2,2,256,256]{3,2,1,0:T(8,128)S(1)}, f32[2,2,256,256]{3,2,1,0:T(8,128)S(1)}, u32[]{:S(2)}, u32[]{:S(2)}) collective-permute-start(f32[2,2,256,256]{3,2,1,0:T(8,128)S(1)} %get-tuple-element.89), channel_id=1, source_target_pairs={{0,2},{1,3},{2,0},{3,1},{4,6},{5,7},{6,4},{7,5},{8,10},{9,11},{10,... | collective-permute-start | bytes 3145736 | tf_op jit(solution)/shard_map/ppermute | solution.py:42
  167.0 26.3 %collective-permute-start.23 = (f32[2,512,256]{2,1,0:T(8,128)S(1)}, f32[2,512,256]{2,1,0:T(8,128)S(1)}, u32[]{:S(2)}, u32[]{:S(2)}) collective-permute-start(f32[2,512,256]{2,1,0:T(8,128)S(1)} %get-tuple-element.92), channel_id=1, source_target_pairs={{0,4},{4,8},{8,12},{1,5},{5,9},{9,13},{2,6},{6,10},{10,14},{3,7},{... | collective-permute-start | bytes 3145736 | tf_op jit(solution)/shard_map/ppermute | solution.py:32
  170.5 38.8 %collective-permute-start.26 = (f32[2,2,256,256]{3,2,1,0:T(8,128)S(1)}, f32[2,2,256,256]{3,2,1,0:T(8,128)S(1)}, u32[]{:S(2)}, u32[]{:S(2)}) collective-permute-start(f32[2,2,256,256]{3,2,1,0:T(8,128)S(1)} %get-tuple-element.95), channel_id=1, source_target_pairs={{0,2},{1,3},{2,0},{3,1},{4,6},{5,7},{6,4},{7,5},{8,10},{9,11},{10,... | collective-permute-start | bytes 3145736 | tf_op jit(solution)/shard_map/ppermute | solution.py:42
  171.1 15.9 %collective-permute-start.18 = (f32[1,2,128,256]{3,2,1,0:T(8,128)S(1)}, f32[1,2,128,256]{3,2,1,0:T(8,128)S(1)}, u32[]{:S(2)}, u32[]{:S(2)}) collective-permute-start(f32[1,2,128,256]{3,2,1,0:T(8,128)S(1)} %get-tuple-element.122), channel_id=1, source_target_pairs={{0,1},{1,0},{2,3},{3,2},{4,5},{5,4},{6,7},{7,6},{8,9},{9,8},{10,11... | collective-permute-start | bytes 786440 | tf_op jit(solution)/shard_map/ppermute | solution.py:37
  171.2 16.4 %collective-permute-start.19 = (f32[1,2,128,256]{3,2,1,0:T(8,128)S(1)}, f32[1,2,128,256]{3,2,1,0:T(8,128)S(1)}, u32[]{:S(2)}, u32[]{:S(2)}) collective-permute-start(f32[1,2,128,256]{3,2,1,0:T(8,128)S(1)} %get-tuple-element.121), channel_id=1, source_target_pairs={{0,1},{1,0},{2,3},{3,2},{4,5},{5,4},{6,7},{7,6},{8,9},{9,8},{10,11... | collective-permute-start | bytes 786440 | tf_op jit(solution)/shard_map/ppermute | solution.py:37
  193.3 28.0 %collective-permute-start.29 = (f32[2,512,256]{2,1,0:T(8,128)S(1)}, f32[2,512,256]{2,1,0:T(8,128)S(1)}, u32[]{:S(2)}, u32[]{:S(2)}) collective-permute-start(f32[2,512,256]{2,1,0:T(8,128)S(1)} %get-tuple-element.98), channel_id=1, source_target_pairs={{0,4},{4,8},{8,12},{1,5},{5,9},{9,13},{2,6},{6,10},{10,14},{3,7},{... | collective-permute-start | bytes 3145736 | tf_op jit(solution)/shard_map/ppermute | solution.py:32
  197.8 11.7 %collective-permute-start.24 = (f32[1,2,128,256]{3,2,1,0:T(8,128)S(1)}, f32[1,2,128,256]{3,2,1,0:T(8,128)S(1)}, u32[]{:S(2)}, u32[]{:S(2)}) collective-permute-start(f32[1,2,128,256]{3,2,1,0:T(8,128)S(1)} %get-tuple-element.118), channel_id=1, source_target_pairs={{0,1},{1,0},{2,3},{3,2},{4,5},{5,4},{6,7},{7,6},{8,9},{9,8},{10,11... | collective-permute-start | bytes 786440 | tf_op jit(solution)/shard_map/ppermute | solution.py:37
  197.8 31.4 %collective-permute-start.32 = (f32[2,2,256,256]{3,2,1,0:T(8,128)S(1)}, f32[2,2,256,256]{3,2,1,0:T(8,128)S(1)}, u32[]{:S(2)}, u32[]{:S(2)}) collective-permute-start(f32[2,2,256,256]{3,2,1,0:T(8,128)S(1)} %get-tuple-element.101), channel_id=1, source_target_pairs={{0,2},{1,3},{2,0},{3,1},{4,6},{5,7},{6,4},{7,5},{8,10},{9,11},{10,... | collective-permute-start | bytes 3145736 | tf_op jit(solution)/shard_map/ppermute | solution.py:42
  198.3 11.6 %collective-permute-start.25 = (f32[1,2,128,256]{3,2,1,0:T(8,128)S(1)}, f32[1,2,128,256]{3,2,1,0:T(8,128)S(1)}, u32[]{:S(2)}, u32[]{:S(2)}) collective-permute-start(f32[1,2,128,256]{3,2,1,0:T(8,128)S(1)} %get-tuple-element.117), channel_id=1, source_target_pairs={{0,1},{1,0},{2,3},{3,2},{4,5},{5,4},{6,7},{7,6},{8,9},{9,8},{10,11... | collective-permute-start | bytes 786440 | tf_op jit(solution)/shard_map/ppermute | solution.py:37
  213.1 29.0 %collective-permute-start.35 = (f32[2,512,256]{2,1,0:T(8,128)S(1)}, f32[2,512,256]{2,1,0:T(8,128)S(1)}, u32[]{:S(2)}, u32[]{:S(2)}) collective-permute-start(f32[2,512,256]{2,1,0:T(8,128)S(1)} %get-tuple-element.105), channel_id=1, source_target_pairs={{0,4},{4,8},{8,12},{1,5},{5,9},{9,13},{2,6},{6,10},{10,14},{3,7},{... | collective-permute-start | bytes 3145736 | tf_op jit(solution)/shard_map/ppermute | solution.py:32
  221.3 8.5 %collective-permute-start.30 = (f32[1,2,128,256]{3,2,1,0:T(8,128)S(1)}, f32[1,2,128,256]{3,2,1,0:T(8,128)S(1)}, u32[]{:S(2)}, u32[]{:S(2)}) collective-permute-start(f32[1,2,128,256]{3,2,1,0:T(8,128)S(1)} %get-tuple-element.114), channel_id=1, source_target_pairs={{0,1},{1,0},{2,3},{3,2},{4,5},{5,4},{6,7},{7,6},{8,9},{9,8},{10,11... | collective-permute-start | bytes 786440 | tf_op jit(solution)/shard_map/ppermute | solution.py:37
  221.4 8.5 %collective-permute-start.31 = (f32[1,2,128,256]{3,2,1,0:T(8,128)S(1)}, f32[1,2,128,256]{3,2,1,0:T(8,128)S(1)}, u32[]{:S(2)}, u32[]{:S(2)}) collective-permute-start(f32[1,2,128,256]{3,2,1,0:T(8,128)S(1)} %get-tuple-element.113), channel_id=1, source_target_pairs={{0,1},{1,0},{2,3},{3,2},{4,5},{5,4},{6,7},{7,6},{8,9},{9,8},{10,11... | collective-permute-start | bytes 786440 | tf_op jit(solution)/shard_map/ppermute | solution.py:37
  242.1 25.4 %collective-permute-start.36 = (f32[2,512,256]{2,1,0:T(8,128)S(1)}, f32[2,512,256]{2,1,0:T(8,128)S(1)}, u32[]{:S(2)}, u32[]{:S(2)}) collective-permute-start(f32[2,512,256]{2,1,0:T(8,128)S(1)} %get-tuple-element.106), channel_id=1, source_target_pairs={{0,4},{4,8},{8,12},{1,5},{5,9},{9,13},{2,6},{6,10},{10,14},{3,7},{... | collective-permute-start | bytes 3145736 | tf_op jit(solution)/shard_map/ppermute | solution.py:32
  (33 other events, 207.6 us)
Sparse Core Ops, SparseCore 0:
  20.0 49.5 all-gather.2
